TPU v7x, 32 devices: a whole 2x2x4 slice. The times are simulated.
32 devices in a mesh: ctx: 8 (over y, x, core), head: 4 (over z).
Axes of the slice: x: 2, y: 2, z: 4, core: 2. Of those that a mesh axis runs over, the one named last changes fastest.
Arguments:
- queries: bfloat16 [32, 16384, 128], P('head', 'ctx'), may hold values from -6 to 6
- key_states: bfloat16 [16, 16384, 128], P('head', 'ctx'), may hold values from -6 to 6
- value_states: bfloat16 [16, 16384, 128], P('head', 'ctx'), may hold values from -6 to 6
- attn_output: bfloat16 [16384, 4096], P(('ctx', 'head')), may hold values from -6 to 6
- out_cotangent: bfloat16 [16384, 4096], P(('ctx', 'head')), may hold values from -6 to 6
- logsumexp: float32 [32, 16384], P('head', 'ctx'), may hold values from 4.5 to 6.5
- doc_start: int32 [16384], P('ctx'), may hold values from 0 to 15360, as said below
Outputs:
- grad_queries: bfloat16 [32, 16384, 128], P('head', 'ctx')
- grad_keys: bfloat16 [16, 16384, 128], P('head', 'ctx')
- grad_values: bfloat16 [16, 16384, 128], P('head', 'ctx')
Inputs may be any that keep to these rules, and one draw needn't show every extreme that they name: doc_start[t] <= t and never falls; each value is the first position of a document; doc_start[0] = 0; the last 1024 positions form one document that starts at 15360; every other document has half of 1024 to 3072 tokens, except that the one just before the last may be shorter.
All inputs are finite; a program needn't handle non-finite values.
Results may differ from a plain program's by a relative error of at most 0.0049.
Values may be sent and summed in bfloat16 or wider, within the bound.
No kernel may reach another device: no remote copies, remote signals or barrier semaphores. Data moves between devices by JAX's collectives and lax.ppermute only.
A program may use at most 192 MiB of HBM per device.

v0:
```python
import jax
import jax.numpy as jnp
from jax import lax
from jax.sharding import PartitionSpec as P

W = 1024
QPRE = 168


def from_behind(block, axis, distance):
    devices = range(lax.axis_size(axis))
    route = [(i - distance, i) for i in devices if i - distance in devices]
    return lax.ppermute(block, axis, route)


def band_tile(
    query_block, cotan_block, lse_block, delta_block, key_block, value_block, allowed, score_scale
):
    scores = (
        jnp.einsum("kgrd,kjd->kgrj", query_block, key_block, preferred_element_type=jnp.float32)
        * score_scale
    )
    probs = jnp.where(allowed, jnp.exp(scores - lse_block[..., None]), jnp.float32(0.0))
    probs_low = probs.astype(jnp.bfloat16)
    dprobs = jnp.einsum(
        "rkgd,kjd->kgrj", cotan_block, value_block, preferred_element_type=jnp.float32
    )
    dscores = (probs * (dprobs - delta_block[..., None])).astype(jnp.bfloat16)
    grad_value = jnp.einsum(
        "kgrj,rkgd->kjd", probs_low, cotan_block, preferred_element_type=jnp.float32
    )
    grad_key = (
        jnp.einsum("kgrj,kgrd->kjd", dscores, query_block, preferred_element_type=jnp.float32)
        * score_scale
    )
    grad_query = (
        jnp.einsum("kgrj,kjd->kgrd", dscores, key_block, preferred_element_type=jnp.float32)
        * score_scale
    )
    return (grad_query, grad_key, grad_value)


def body(queries, key_states, value_states, attn_output, out_cotangent, logsumexp, doc_start):
    kv_heads, tok_rows, head_dim = key_states.shape
    q_heads = queries.shape[0]
    groups = q_heads // kv_heads
    window = W
    block_rows = min(512, tok_rows)
    n_blocks = tok_rows // block_rows
    span = block_rows + window
    score_scale = QPRE ** (-0.5)
    shard_base = lax.axis_index("ctx") * tok_rows
    total_heads = out_cotangent.shape[1] // head_dim
    seq_cotan = out_cotangent.reshape(out_cotangent.shape[0], total_heads, head_dim)
    seq_output = attn_output.reshape(attn_output.shape[0], total_heads, head_dim)
    cotan_heads, output_heads = (
        lax.all_to_all(seq_cotan, "head", split_axis=1, concat_axis=0, tiled=True),
        lax.all_to_all(seq_output, "head", split_axis=1, concat_axis=0, tiled=True),
    )
    row_delta = jnp.sum(cotan_heads.astype(jnp.float32) * output_heads.astype(jnp.float32), axis=2)
    delta_grouped = row_delta.reshape(tok_rows, kv_heads, groups).transpose(1, 2, 0)
    lse_grouped = logsumexp.reshape(kv_heads, groups, tok_rows)
    query_grouped = queries.reshape(kv_heads, groups, tok_rows, head_dim)
    key_rim, value_rim = from_behind(
        (key_states[:, tok_rows - window :], value_states[:, tok_rows - window :]), "ctx", 1
    )
    key_ext = jnp.concatenate([key_rim, key_states], axis=1)
    value_ext = jnp.concatenate([value_rim, value_states], axis=1)
    row_iota = jnp.arange(block_rows, dtype=jnp.int32)
    col_iota = jnp.arange(span, dtype=jnp.int32)
    distance = row_iota[:, None] + window - col_iota[None, :]
    near = (distance >= 0) & (distance < window)

    def block_step(index, carry):
        grad_key_ext, grad_value_ext, grad_query_all = carry
        first = index * block_rows
        query_block = lax.dynamic_slice_in_dim(query_grouped, first, block_rows, 2)
        lse_block = lax.dynamic_slice_in_dim(lse_grouped, first, block_rows, 2)
        delta_block = lax.dynamic_slice_in_dim(delta_grouped, first, block_rows, 2)
        cotan_block = lax.dynamic_slice_in_dim(cotan_heads, first, block_rows, 0).reshape(
            block_rows, kv_heads, groups, head_dim
        )
        key_block = lax.dynamic_slice_in_dim(key_ext, first, span, 1)
        value_block = lax.dynamic_slice_in_dim(value_ext, first, span, 1)
        start_rel = lax.dynamic_slice_in_dim(doc_start, first, block_rows, 0) - shard_base
        key_local = first - window + col_iota
        allowed = near & (key_local[None, :] >= start_rel[:, None])
        grad_query, grad_key, grad_value = band_tile(
            query_block,
            cotan_block,
            lse_block,
            delta_block,
            key_block,
            value_block,
            allowed,
            score_scale,
        )
        grad_key_ext = lax.dynamic_update_slice_in_dim(
            grad_key_ext,
            lax.dynamic_slice_in_dim(grad_key_ext, first, span, 1) + grad_key,
            first,
            1,
        )
        grad_value_ext = lax.dynamic_update_slice_in_dim(
            grad_value_ext,
            lax.dynamic_slice_in_dim(grad_value_ext, first, span, 1) + grad_value,
            first,
            1,
        )
        grad_query_all = lax.dynamic_update_slice_in_dim(
            grad_query_all, grad_query.astype(jnp.bfloat16), first, 2
        )
        return (grad_key_ext, grad_value_ext, grad_query_all)

    initial = (
        jnp.zeros((kv_heads, tok_rows + window, head_dim), jnp.float32),
        jnp.zeros((kv_heads, tok_rows + window, head_dim), jnp.float32),
        jnp.zeros((kv_heads, groups, tok_rows, head_dim), jnp.bfloat16),
    )
    grad_key_ext, grad_value_ext, grad_query_all = lax.fori_loop(0, n_blocks, block_step, initial)
    back_key, back_value = from_behind(
        (grad_key_ext[:, :window], grad_value_ext[:, :window]), "ctx", -1
    )
    own_key = grad_key_ext[:, window:]
    own_value = grad_value_ext[:, window:]
    grad_keys = jnp.concatenate(
        [own_key[:, : tok_rows - window], own_key[:, tok_rows - window :] + back_key], axis=1
    )
    grad_values = jnp.concatenate(
        [own_value[:, : tok_rows - window], own_value[:, tok_rows - window :] + back_value], axis=1
    )
    grad_queries = grad_query_all.reshape(q_heads, tok_rows, head_dim)
    return (grad_queries, grad_keys.astype(jnp.bfloat16), grad_values.astype(jnp.bfloat16))


def solution(mesh):
    return jax.shard_map(
        body,
        mesh=mesh,
        in_specs=(
            P("head", "ctx", None),
            P("head", "ctx", None),
            P("head", "ctx", None),
            P(("ctx", "head"), None),
            P(("ctx", "head"), None),
            P("head", "ctx"),
            P("ctx"),
        ),
        out_specs=(P("head", "ctx", None), P("head", "ctx", None), P("head", "ctx", None)),
        check_vma=False,
    )
```

profile of v0, /device:TPU:1, one launch (start us, length us, event | category | flops | bytes accessed | tf_op | source)
XLA Modules:
  0.0 551.3 jit_solution(12323824536151723759)
XLA Ops:
  31.8 79.9 %all-to-all-done.1 = bf16[512,32,128]{2,0,1:T(8,128)(2,1)} async-done(((bf16[512,32,128]{2,0,1:T(8,128)(2,1)}), bf16[512,32,128]{2,0,1:T(8,128)(2,1)}, u32[]{:S(2)}, u32[]{:S(2)}) %all-to-all-start.1) | async-done | bytes 4194336 | tf_op jit(solution)/shard_map/all_to_all | solution.py:58
  148.5 60.7 %all-to-all-done = bf16[512,32,128]{2,0,1:T(8,128)(2,1)} async-done(((bf16[512,32,128]{2,0,1:T(8,128)(2,1)}), bf16[512,32,128]{2,0,1:T(8,128)(2,1)}, u32[]{:S(2)}, u32[]{:S(2)}) %all-to-all-start) | async-done | bytes 4194336 | tf_op jit(solution)/shard_map/all_to_all | solution.py:57
  209.3 9.6 %fusion.38 = f32[4,512,8]{2,0,1:T(4,128)S(1)} fusion(bf16[512,32,128]{2,0,1:T(8,128)(2,1)} %all-to-all-done.1, bf16[512,32,128]{2,0,1:T(8,128)(2,1)} %all-to-all-done), kind=kLoop, calls=%fused_computation.40 | loop fusion | flops 8372224 | bytes 8454144 | tf_op jit(solution)/shard_map/reduce_sum | solution.py:60
  234.9 262.0 %while.20 = (s32[]{:T(128)}, f32[4,3072,128]{2,1,0:T(8,128)}, f32[4,3072,128]{2,1,0:T(8,128)}, bf16[4,2,2048,128]{3,2,1,0:T(8,128)(2,1)}, s32[2048]{0:T(1024)}, ...) while((s32[]{:T(128)}, f32[4,3072,128]{2,1,0:T(8,128)}, ...), condition=%wide.region_2.3_spmd.clone, body=%wide.region_1.2_spmd.clone.sunk | while | flops 8105232384 | bytes 154259824 | solution.py:120
  238.5 12.6 %exponential_select_fusion.2 = f32[4,2,512,1536]{3,2,1,0:T(8,128)} fusion(f32[4,2,512]{2,1,0:T(2,128)S(1)} %get-tuple-element.516, pred[512,1536]{1,0:T(8,128)(4,1)S(1)} %fusion.67, bf16[4,3072,128]{2,1,0:T(8,128)(2,1)S(1)} %copy-done.3, s32[]{:T(128)S(6)} %select_n.49, bf16[4,2,2048,128]{3,2,1,0:T(8,128)(2,1)} %get-tuple-element.562, s32[]{:T(128)S(6)} %select_n.50), kind=kOutput, calls=%fused_computation.5.clone.1 | convolution fusion | flops 1629487104 | bytes 28590088 | tf_op jit(solution)/shard_map/while/body/eval_jaxpr/kgrd,kjd->kgrj/dot_general | solution.py:20
  251.1 13.1 %fusion.69 = f32[4,3072,128]{2,1,0:T(8,128)} fusion(f32[4,3072,128]{2,1,0:T(8,128)} %get-tuple-element.539, s32[]{:T(128)S(6)} %select_n.49, bf16[512,4,2,128]{3,0,2,1:T(8,128)(2,1)S(1)} %bitcast.83, f32[4,2,512,1536]{3,2,1,0:T(8,128)} %exponential_select_fusion.2), kind=kOutput, calls=%fused_computation.11.clone.1 | convolution fusion | flops 1617690624 | bytes 32505860 | tf_op jit(solution)/shard_map/while/body/eval_jaxpr/kgrj,rkgd->kjd/dot_general | solution.py:29
  264.2 15.0 %fusion.68 = bf16[4,2,512,1536]{3,2,1,0:T(8,128)(2,1)} fusion(f32[4,2,512,1536]{3,2,1,0:T(8,128)} %exponential_select_fusion.2, bf16[512,4,2,128]{3,0,2,1:T(8,128)(2,1)S(1)} %bitcast.84, f32[4,2,512]{2,1,0:T(2,128)S(1)} %get-tuple-element.517, bf16[4,3072,128]{2,1,0:T(8,128)(2,1)} %get-tuple-element.565, s32[]{:T(128)S(6)} %select_n.49), kind=kOutput, calls=%fused_computation.4.clone.1 | convolution fusion | flops 1629487104 | bytes 40386564 | tf_op jit(solution)/shard_map/while/body/eval_jaxpr/rkgd,kjd->kgrj/dot_general | solution.py:25
  279.2 9.4 %fusion.70 = bf16[4,2,2048,128]{3,2,1,0:T(8,128)(2,1)} fusion(bf16[4,2,2048,128]{3,2,1,0:T(8,128)(2,1)} %get-tuple-element.540, s32[]{:T(128)S(6)} %select_n.50, bf16[4,2,512,1536]{3,2,1,0:T(8,128)(2,1)} %fusion.68, bf16[4,3072,128]{2,1,0:T(8,128)(2,1)} %get-tuple-element.563, s32[]{:T(128)S(6)} %select_n.49), kind=kOutput, calls=%fused_computation.24.clone.1 | convolution fusion | flops 1611661312 | bytes 15204360 | tf_op jit(solution)/shard_map/while/body/eval_jaxpr/kgrj,kjd->kgrd/dot_general | solution.py:37
  288.6 11.8 %add_dynamic-update-slice_fusion.2 = f32[4,3072,128]{2,1,0:T(8,128)} fusion(f32[4,3072,128]{2,1,0:T(8,128)} %get-tuple-element.538, s32[]{:T(128)S(6)} %select_n.49, bf16[4,2,512,1536]{3,2,1,0:T(8,128)(2,1)} %fusion.68, bf16[4,2,2048,128]{3,2,1,0:T(8,128)(2,1)} %get-tuple-element.562, s32[]{:T(128)S(6)} %select_n.50), kind=kOutput, calls=%fused_computation.16.clone.1 | convolution fusion | flops 1612185600 | bytes 19922952 | tf_op jit(solution)/shard_map/while/body/eval_jaxpr/kgrj,kgrd->kjd/dot_general | solution.py:33
  304.0 12.6 %exponential_select_fusion.2 = f32[4,2,512,1536]{3,2,1,0:T(8,128)} fusion(f32[4,2,512]{2,1,0:T(2,128)S(1)} %get-tuple-element.516, pred[512,1536]{1,0:T(8,128)(4,1)S(1)} %fusion.67, bf16[4,3072,128]{2,1,0:T(8,128)(2,1)S(1)} %copy-done.3, s32[]{:T(128)S(6)} %select_n.49, bf16[4,2,2048,128]{3,2,1,0:T(8,128)(2,1)} %get-tuple-element.562, s32[]{:T(128)S(6)} %select_n.50), kind=kOutput, calls=%fused_computation.5.clone.1 | convolution fusion | flops 1629487104 | bytes 28590088 | tf_op jit(solution)/shard_map/while/body/eval_jaxpr/kgrd,kjd->kgrj/dot_general | solution.py:20
  316.6 13.1 %fusion.69 = f32[4,3072,128]{2,1,0:T(8,128)} fusion(f32[4,3072,128]{2,1,0:T(8,128)} %get-tuple-element.539, s32[]{:T(128)S(6)} %select_n.49, bf16[512,4,2,128]{3,0,2,1:T(8,128)(2,1)S(1)} %bitcast.83, f32[4,2,512,1536]{3,2,1,0:T(8,128)} %exponential_select_fusion.2), kind=kOutput, calls=%fused_computation.11.clone.1 | convolution fusion | flops 1617690624 | bytes 32505860 | tf_op jit(solution)/shard_map/while/body/eval_jaxpr/kgrj,rkgd->kjd/dot_general | solution.py:29
  329.7 15.0 %fusion.68 = bf16[4,2,512,1536]{3,2,1,0:T(8,128)(2,1)} fusion(f32[4,2,512,1536]{3,2,1,0:T(8,128)} %exponential_select_fusion.2, bf16[512,4,2,128]{3,0,2,1:T(8,128)(2,1)S(1)} %bitcast.84, f32[4,2,512]{2,1,0:T(2,128)S(1)} %get-tuple-element.517, bf16[4,3072,128]{2,1,0:T(8,128)(2,1)} %get-tuple-element.565, s32[]{:T(128)S(6)} %select_n.49), kind=kOutput, calls=%fused_computation.4.clone.1 | convolution fusion | flops 1629487104 | bytes 40386564 | tf_op jit(solution)/shard_map/while/body/eval_jaxpr/rkgd,kjd->kgrj/dot_general | solution.py:25
  344.7 9.4 %fusion.70 = bf16[4,2,2048,128]{3,2,1,0:T(8,128)(2,1)} fusion(bf16[4,2,2048,128]{3,2,1,0:T(8,128)(2,1)} %get-tuple-element.540, s32[]{:T(128)S(6)} %select_n.50, bf16[4,2,512,1536]{3,2,1,0:T(8,128)(2,1)} %fusion.68, bf16[4,3072,128]{2,1,0:T(8,128)(2,1)} %get-tuple-element.563, s32[]{:T(128)S(6)} %select_n.49), kind=kOutput, calls=%fused_computation.24.clone.1 | convolution fusion | flops 1611661312 | bytes 15204360 | tf_op jit(solution)/shard_map/while/body/eval_jaxpr/kgrj,kjd->kgrd/dot_general | solution.py:37
  354.1 11.8 %add_dynamic-update-slice_fusion.2 = f32[4,3072,128]{2,1,0:T(8,128)} fusion(f32[4,3072,128]{2,1,0:T(8,128)} %get-tuple-element.538, s32[]{:T(128)S(6)} %select_n.49, bf16[4,2,512,1536]{3,2,1,0:T(8,128)(2,1)} %fusion.68, bf16[4,2,2048,128]{3,2,1,0:T(8,128)(2,1)} %get-tuple-element.562, s32[]{:T(128)S(6)} %select_n.50), kind=kOutput, calls=%fused_computation.16.clone.1 | convolution fusion | flops 1612185600 | bytes 19922952 | tf_op jit(solution)/shard_map/while/body/eval_jaxpr/kgrj,kgrd->kjd/dot_general | solution.py:33
  369.5 12.5 %exponential_select_fusion.2 = f32[4,2,512,1536]{3,2,1,0:T(8,128)} fusion(f32[4,2,512]{2,1,0:T(2,128)S(1)} %get-tuple-element.516, pred[512,1536]{1,0:T(8,128)(4,1)S(1)} %fusion.67, bf16[4,3072,128]{2,1,0:T(8,128)(2,1)S(1)} %copy-done.3, s32[]{:T(128)S(6)} %select_n.49, bf16[4,2,2048,128]{3,2,1,0:T(8,128)(2,1)} %get-tuple-element.562, s32[]{:T(128)S(6)} %select_n.50), kind=kOutput, calls=%fused_computation.5.clone.1 | convolution fusion | flops 1629487104 | bytes 28590088 | tf_op jit(solution)/shard_map/while/body/eval_jaxpr/kgrd,kjd->kgrj/dot_general | solution.py:20
  382.1 13.1 %fusion.69 = f32[4,3072,128]{2,1,0:T(8,128)} fusion(f32[4,3072,128]{2,1,0:T(8,128)} %get-tuple-element.539, s32[]{:T(128)S(6)} %select_n.49, bf16[512,4,2,128]{3,0,2,1:T(8,128)(2,1)S(1)} %bitcast.83, f32[4,2,512,1536]{3,2,1,0:T(8,128)} %exponential_select_fusion.2), kind=kOutput, calls=%fused_computation.11.clone.1 | convolution fusion | flops 1617690624 | bytes 32505860 | tf_op jit(solution)/shard_map/while/body/eval_jaxpr/kgrj,rkgd->kjd/dot_general | solution.py:29
  395.2 15.0 %fusion.68 = bf16[4,2,512,1536]{3,2,1,0:T(8,128)(2,1)} fusion(f32[4,2,512,1536]{3,2,1,0:T(8,128)} %exponential_select_fusion.2, bf16[512,4,2,128]{3,0,2,1:T(8,128)(2,1)S(1)} %bitcast.84, f32[4,2,512]{2,1,0:T(2,128)S(1)} %get-tuple-element.517, bf16[4,3072,128]{2,1,0:T(8,128)(2,1)} %get-tuple-element.565, s32[]{:T(128)S(6)} %select_n.49), kind=kOutput, calls=%fused_computation.4.clone.1 | convolution fusion | flops 1629487104 | bytes 40386564 | tf_op jit(solution)/shard_map/while/body/eval_jaxpr/rkgd,kjd->kgrj/dot_general | solution.py:25
  419.6 11.8 %add_dynamic-update-slice_fusion.2 = f32[4,3072,128]{2,1,0:T(8,128)} fusion(f32[4,3072,128]{2,1,0:T(8,128)} %get-tuple-element.538, s32[]{:T(128)S(6)} %select_n.49, bf16[4,2,512,1536]{3,2,1,0:T(8,128)(2,1)} %fusion.68, bf16[4,2,2048,128]{3,2,1,0:T(8,128)(2,1)} %get-tuple-element.562, s32[]{:T(128)S(6)} %select_n.50), kind=kOutput, calls=%fused_computation.16.clone.1 | convolution fusion | flops 1612185600 | bytes 19922952 | tf_op jit(solution)/shard_map/while/body/eval_jaxpr/kgrj,kgrd->kjd/dot_general | solution.py:33
  435.1 12.6 %exponential_select_fusion.2 = f32[4,2,512,1536]{3,2,1,0:T(8,128)} fusion(f32[4,2,512]{2,1,0:T(2,128)S(1)} %get-tuple-element.516, pred[512,1536]{1,0:T(8,128)(4,1)S(1)} %fusion.67, bf16[4,3072,128]{2,1,0:T(8,128)(2,1)S(1)} %copy-done.3, s32[]{:T(128)S(6)} %select_n.49, bf16[4,2,2048,128]{3,2,1,0:T(8,128)(2,1)} %get-tuple-element.562, s32[]{:T(128)S(6)} %select_n.50), kind=kOutput, calls=%fused_computation.5.clone.1 | convolution fusion | flops 1629487104 | bytes 28590088 | tf_op jit(solution)/shard_map/while/body/eval_jaxpr/kgrd,kjd->kgrj/dot_general | solution.py:20
  447.6 13.1 %fusion.69 = f32[4,3072,128]{2,1,0:T(8,128)} fusion(f32[4,3072,128]{2,1,0:T(8,128)} %get-tuple-element.539, s32[]{:T(128)S(6)} %select_n.49, bf16[512,4,2,128]{3,0,2,1:T(8,128)(2,1)S(1)} %bitcast.83, f32[4,2,512,1536]{3,2,1,0:T(8,128)} %exponential_select_fusion.2), kind=kOutput, calls=%fused_computation.11.clone.1 | convolution fusion | flops 1617690624 | bytes 32505860 | tf_op jit(solution)/shard_map/while/body/eval_jaxpr/kgrj,rkgd->kjd/dot_general | solution.py:29
  460.7 15.0 %fusion.68 = bf16[4,2,512,1536]{3,2,1,0:T(8,128)(2,1)} fusion(f32[4,2,512,1536]{3,2,1,0:T(8,128)} %exponential_select_fusion.2, bf16[512,4,2,128]{3,0,2,1:T(8,128)(2,1)S(1)} %bitcast.84, f32[4,2,512]{2,1,0:T(2,128)S(1)} %get-tuple-element.517, bf16[4,3072,128]{2,1,0:T(8,128)(2,1)} %get-tuple-element.565, s32[]{:T(128)S(6)} %select_n.49), kind=kOutput, calls=%fused_computation.4.clone.1 | convolution fusion | flops 1629487104 | bytes 40386564 | tf_op jit(solution)/shard_map/while/body/eval_jaxpr/rkgd,kjd->kgrj/dot_general | solution.py:25
  485.1 11.8 %add_dynamic-update-slice_fusion.2 = f32[4,3072,128]{2,1,0:T(8,128)} fusion(f32[4,3072,128]{2,1,0:T(8,128)} %get-tuple-element.538, s32[]{:T(128)S(6)} %select_n.49, bf16[4,2,512,1536]{3,2,1,0:T(8,128)(2,1)} %fusion.68, bf16[4,2,2048,128]{3,2,1,0:T(8,128)(2,1)} %get-tuple-element.562, s32[]{:T(128)S(6)} %select_n.50), kind=kOutput, calls=%fused_computation.16.clone.1 | convolution fusion | flops 1612185600 | bytes 19922952 | tf_op jit(solution)/shard_map/while/body/eval_jaxpr/kgrj,kgrd->kjd/dot_general | solution.py:33
  507.9 19.3 %collective-permute-done.3 = f32[4,1024,128]{2,1,0:T(8,128)S(1)} collective-permute-done((f32[4,1024,128]{2,1,0:T(8,128)S(1)}, f32[4,1024,128]{2,1,0:T(8,128)S(1)}, u32[]{:S(2)}, u32[]{:S(2)}) %collective-permute-start.3) | collective-permute-done | bytes 2097184 | tf_op jit(solution)/shard_map/ppermute | solution.py:13
  530.5 19.2 %collective-permute-done.2 = f32[4,1024,128]{2,1,0:T(8,128)S(1)} collective-permute-done((f32[4,1024,128]{2,1,0:T(8,128)S(1)}, f32[4,1024,128]{2,1,0:T(8,128)S(1)}, u32[]{:S(2)}, u32[]{:S(2)}) %collective-permute-start.2) | collective-permute-done | bytes 2097184 | tf_op jit(solution)/shard_map/ppermute | solution.py:13
  (74 shorter events, 133.0 us)
Async XLA Ops:
  13.5 98.2 %all-to-all-start.1 = ((bf16[512,32,128]{2,0,1:T(8,128)(2,1)}), bf16[512,32,128]{2,0,1:T(8,128)(2,1)}, u32[]{:S(2)}, u32[]{:S(2)}) async-start(bf16[512,32,128]{2,0,1:T(8,128)(2,1)} %copy.36), calls=%async_computation.1 | async-start | bytes 8388608 | tf_op jit(solution)/shard_map/all_to_all | solution.py:58
  31.8 84.8 %copy-start.1 = (bf16[4,2048,128]{2,1,0:T(8,128)(2,1)S(1)}, bf16[4,2048,128]{2,1,0:T(8,128)(2,1)}, u32[]{:S(2)}) copy-start(bf16[4,2048,128]{2,1,0:T(8,128)(2,1)} %param.10) | copy-start | bytes 6291460
  111.7 97.5 %all-to-all-start = ((bf16[512,32,128]{2,0,1:T(8,128)(2,1)}), bf16[512,32,128]{2,0,1:T(8,128)(2,1)}, u32[]{:S(2)}, u32[]{:S(2)}) async-start(bf16[512,32,128]{2,0,1:T(8,128)(2,1)} %copy.32), calls=%async_computation | async-start | bytes 8388608 | tf_op jit(solution)/shard_map/all_to_all | solution.py:57
  116.6 8.9 %copy-start.4 = (f32[8,2048]{1,0:T(8,128)S(1)}, f32[8,2048]{1,0:T(8,128)}, u32[]{:S(2)}) copy-start(f32[8,2048]{1,0:T(8,128)} %param.14) | copy-start | bytes 196612
  117.6 16.6 %collective-permute-start = (bf16[4,1024,128]{2,1,0:T(8,128)(2,1)}, bf16[4,1024,128]{2,1,0:T(8,128)(2,1)}, u32[]{:S(2)}, u32[]{:S(2)}) collective-permute-start(bf16[4,1024,128]{2,1,0:T(8,128)(2,1)} %slice.32), channel_id=1, source_target_pairs={{0,4},{4,8},{8,12},{12,16},{16,20},{20,24},{24,28},{1,5},{5,9},{9,... | collective-permute-start | bytes 3145736 | tf_op jit(solution)/shard_map/ppermute | solution.py:13
  123.5 21.9 %collective-permute-start.1 = (bf16[4,1024,128]{2,1,0:T(8,128)(2,1)S(1)}, bf16[4,1024,128]{2,1,0:T(8,128)(2,1)}, u32[]{:S(2)}, u32[]{:S(2)}) collective-permute-start(bf16[4,1024,128]{2,1,0:T(8,128)(2,1)S(1)} %slice.33), channel_id=1, source_target_pairs={{0,4},{4,8},{8,12},{12,16},{16,20},{20,24},{24,28},{1,5},{5,9},{9,... | collective-permute-start | bytes 3145736 | tf_op jit(solution)/shard_map/ppermute | solution.py:13
  125.5 19.9 %copy-start.2 = (bf16[4,2048,128]{2,1,0:T(8,128)(2,1)S(1)}, bf16[4,2048,128]{2,1,0:T(8,128)(2,1)}, u32[]{:S(2)}) copy-start(bf16[4,2048,128]{2,1,0:T(8,128)(2,1)} %param.11) | copy-start | bytes 6291460
  234.9 3.7 copy-start.3
  300.3 3.7 copy-start.3
  365.9 3.7 copy-start.3
  431.4 3.7 copy-start.3
  496.9 9.1 %copy-start = (f32[4,3072,128]{2,1,0:T(8,128)S(1)}, f32[4,3072,128]{2,1,0:T(8,128)}, u32[]{:S(2)}) copy-start(f32[4,3072,128]{2,1,0:T(8,128)} %get-tuple-element.336) | copy-start | bytes 18874372
  498.8 28.4 %collective-permute-start.3 = (f32[4,1024,128]{2,1,0:T(8,128)S(1)}, f32[4,1024,128]{2,1,0:T(8,128)S(1)}, u32[]{:S(2)}, u32[]{:S(2)}) collective-permute-start(f32[4,1024,128]{2,1,0:T(8,128)S(1)} %slice.39), channel_id=1, source_target_pairs={{4,0},{8,4},{12,8},{16,12},{20,16},{24,20},{28,24},{5,1},{9,5},{13... | collective-permute-start | bytes 6291464 | tf_op jit(solution)/shard_map/ppermute | solution.py:13
  504.0 45.6 %collective-permute-start.2 = (f32[4,1024,128]{2,1,0:T(8,128)S(1)}, f32[4,1024,128]{2,1,0:T(8,128)S(1)}, u32[]{:S(2)}, u32[]{:S(2)}) collective-permute-start(f32[4,1024,128]{2,1,0:T(8,128)S(1)} %slice.36), channel_id=1, source_target_pairs={{4,0},{8,4},{12,8},{16,12},{20,16},{24,20},{28,24},{5,1},{9,5},{13... | collective-permute-start | bytes 6291464 | tf_op jit(solution)/shard_map/ppermute | solution.py:13
where the time goes:
time: 553 us; the launch traced here: 551 us
  matrix products  247 us (45%)
  waiting for transfers between devices  196 us (35%)
  local copies, waits for them, and re-layouts  55.4 us (10%)
  other arithmetic  29.6 us (5%)
  starting transfers between devices  22.2 us (4%)
    all_to_all x1, waiting for transfers between devices, body(): lax.all_to_all(seq_output, 'head', split_axis=1, concat_axis=0, tiled=True)  79.9 us
    all_to_all x1, waiting for transfers between devices, body(): lax.all_to_all(seq_cotan, 'head', split_axis=1, concat_axis=0, tiled=True)  60.7 us
    dot_general x4, matrix products, band_tile(): jnp.einsum('rkgd,kjd->kgrj', cotan_block, value_block, preferred_element_...  60.1 us
    ppermute x4, waiting for transfers between devices, from_behind(): return lax.ppermute(block, axis, route)  55.3 us
    dot_general x4, matrix products, band_tile(): jnp.einsum('kgrj,rkgd->kjd', probs_low, cotan_block, preferred_element_ty...  52.4 us
    dot_general x4, matrix products, band_tile(): jnp.einsum('kgrd,kjd->kgrj', query_block, key_block, preferred_element_ty...  50.2 us
    dot_general x4, matrix products, band_tile(): jnp.einsum('kgrj,kgrd->kjd', dscores, query_block, preferred_element_type...  47.1 us
    dot_general x4, matrix products, band_tile(): jnp.einsum('kgrj,kjd->kgrd', dscores, key_block, preferred_element_type=j...  37.5 us
  transfers between devices with their start and end apart: 6, of which 6 were waited for; matrix products, arithmetic and copies ran while one was open for 5% of the time, Pallas kernels for 0%

commit v1 on v0

v1 whole, which is shorter than its diff:
```python
import functools
import math

import jax
import jax.numpy as jnp
from jax import lax
from jax.experimental import pallas as pl
from jax.experimental.pallas import tpu as pltpu
from jax.sharding import PartitionSpec as P

W = 1024
QPRE = 168
BLOCK = 128
LOG2E = math.log2(math.e)
F32 = jnp.float32
BF16 = jnp.bfloat16
NT = (((1,), (1,)), ((), ()))
NN = (((1,), (0,)), ((), ()))


def from_behind(block, axis, distance):
    devices = range(lax.axis_size(axis))
    route = [(i - distance, i) for i in devices if i - distance in devices]
    return lax.ppermute(block, axis, route)


def delta_kernel(cotan_ref, output_ref, delta_ref):
    rows, width = cotan_ref.shape
    heads = delta_ref.shape[0]
    product = cotan_ref[...].astype(F32) * output_ref[...].astype(F32)
    high = product.astype(BF16)
    low = (product - high.astype(F32)).astype(BF16)
    head_of = lax.broadcasted_iota(jnp.int32, (heads, width), 1) // (width // heads)
    member = (head_of == lax.broadcasted_iota(jnp.int32, (heads, width), 0)).astype(BF16)
    total = lax.dot_general(member, high, NT, preferred_element_type=F32)
    delta_ref[...] = total + lax.dot_general(member, low, NT, preferred_element_type=F32)


def row_deltas(cotan, output, heads):
    rows, width = cotan.shape
    step = min(128, rows)
    return pl.pallas_call(
        delta_kernel,
        grid=(rows // step,),
        in_specs=[pl.BlockSpec((step, width), lambda i: (i, 0))] * 2,
        out_specs=pl.BlockSpec((heads, step), lambda i: (0, i)),
        out_shape=jax.ShapeDtypeStruct((heads, rows), F32),
        cost_estimate=pl.CostEstimate(
            flops=4 * rows * width * heads, bytes_accessed=4 * rows * width, transcendentals=0
        ),
        name="row_deltas",
    )(cotan, output)


def head_kernel(head, pieces, aliased, me_ref, *refs):
    refs = list(refs)
    q_ref, kh_ref, ko_ref, vh_ref, vo_ref, lse_ref, start_ref = refs[:7]
    cotan_refs = refs[7 : 7 + pieces]
    delta_refs = refs[7 + pieces : 7 + 2 * pieces]
    rest = refs[7 + 2 * pieces + aliased :]
    dq_ref, dk_ref, dv_ref, dk_tail_ref, dv_tail_ref, halo_ref = rest[:6]
    k_all, v_all, kt_all, dk_all, dv_all, ds_all = rest[6:]
    step = pl.program_id(0)
    steps = pl.num_programs(0)
    window = kh_ref.shape[1]
    groups = q_ref.shape[0]
    span = window + BLOCK
    cols = groups * BLOCK
    scale = QPRE ** (-0.5)

    @pl.when(step == 0)
    def _():
        k_all[:window] = kh_ref[0]
        k_all[window:] = ko_ref[0]
        v_all[:window] = vh_ref[0]
        v_all[window:] = vo_ref[0]
        for i in range(k_all.shape[0] // BLOCK):
            rows = pl.ds(i * BLOCK, BLOCK)
            kt_all[:, rows] = k_all[rows, :].T
        dk_all[...] = jnp.zeros_like(dk_all)
        dv_all[...] = jnp.zeros_like(dv_all)

    first = pl.multiple_of(step * BLOCK, BLOCK)
    piece_rows = steps * BLOCK // pieces
    source = lax.rem(me_ref[0] - first // piece_rows + pieces, pieces)

    def pick(options):
        got = options[0]
        for i in range(1, pieces):
            got = jnp.where(source == i, options[i], got)
        return got

    def row_of(block):
        return jnp.concatenate([block[groups * head + i][None] for i in range(groups)], axis=1)

    query = q_ref[...].reshape(cols, q_ref.shape[2])
    cotan = pick([r[...] for r in cotan_refs])
    width = cotan.shape[1] // groups
    cotan = jnp.concatenate([cotan[:, i * width : (i + 1) * width] for i in range(groups)], axis=0)
    delta = row_of(pick([r[...] for r in delta_refs]))
    lse = row_of(lse_ref[...]) * F32(LOG2E)
    start = jnp.concatenate([start_ref[...]] * groups, axis=1) - first
    place = lax.broadcasted_iota(jnp.int32, (BLOCK, cols), 0)
    token = lax.broadcasted_iota(jnp.int32, (BLOCK, cols), 1) % BLOCK

    for i in range(span // BLOCK):
        rows = pl.ds(pl.multiple_of(first + i * BLOCK, BLOCK), BLOCK)
        scores = lax.dot_general(k_all[rows, :], query, NT, preferred_element_type=F32)
        dprobs = lax.dot_general(v_all[rows, :], cotan, NT, preferred_element_type=F32)
        allowed = place >= start - i * BLOCK
        if i == 0:
            allowed = allowed & (place > token)
        if i == span // BLOCK - 1:
            allowed = allowed & (place <= token)
        probs = jnp.where(allowed, jnp.exp2(scores * F32(scale * LOG2E) - lse), F32(0.0))
        dscores = (probs * (dprobs - delta)).astype(BF16)
        ds_all[i * BLOCK : (i + 1) * BLOCK, :] = dscores
        dv_all[rows, :] += lax.dot_general(probs.astype(BF16), cotan, NN, preferred_element_type=F32)
        dk_all[rows, :] += lax.dot_general(dscores, query, NN, preferred_element_type=F32)
    dq = lax.dot_general(
        kt_all[:, pl.ds(first, span)], ds_all[...], NN, preferred_element_type=F32
    )
    dq_ref[...] = (dq.T * F32(scale)).astype(BF16).reshape(dq_ref.shape)

    @pl.when(step == steps - 1)
    def _():
        own = dk_ref.shape[1]
        halo_ref[0] = (dk_all[:window] * F32(scale)).astype(BF16)
        halo_ref[1] = dv_all[:window].astype(BF16)
        dk_ref[0] = (dk_all[window : window + own] * F32(scale)).astype(BF16)
        dv_ref[0] = dv_all[window : window + own].astype(BF16)
        dk_tail_ref[...] = dk_all[window + own :] * F32(scale)
        dv_tail_ref[...] = dv_all[window + own :]


def head_call(head, me, queries, key_rim, keys, value_rim, values, lse, start, cotans, deltas, before):
    kv_heads, tok_rows, head_dim = keys.shape
    q_heads = queries.shape[0]
    groups = q_heads // kv_heads
    window = key_rim.shape[1]
    pieces = len(cotans)
    steps = tok_rows // BLOCK
    in_piece = steps // pieces
    own = tok_rows - window
    cols = groups * head_dim
    ext = tok_rows + window
    whole = pl.BlockSpec((1, tok_rows, head_dim), lambda i, me: (head, 0, 0))
    rim = pl.BlockSpec((1, window, head_dim), lambda i, me: (head, 0, 0))
    in_specs = [
        pl.BlockSpec((groups, BLOCK, head_dim), lambda i, me: (head, i, 0)),
        rim,
        whole,
        rim,
        whole,
        pl.BlockSpec((q_heads, BLOCK), lambda i, me: (0, i)),
        pl.BlockSpec((1, BLOCK), lambda i, me: (0, i)),
    ]
    in_specs += [pl.BlockSpec((BLOCK, cols), lambda i, me: (lax.rem(i, in_piece), 0))] * pieces
    in_specs += [pl.BlockSpec((q_heads, BLOCK), lambda i, me: (0, lax.rem(i, in_piece)))] * pieces
    in_specs += [pl.BlockSpec(memory_space=pl.ANY)] * len(before)
    n_in = 1 + 7 + 2 * pieces
    out_specs = [
        pl.BlockSpec((groups, BLOCK, head_dim), lambda i, me: (head, i, 0)),
        pl.BlockSpec((1, own, head_dim), lambda i, me: (head, 0, 0)),
        pl.BlockSpec((1, own, head_dim), lambda i, me: (head, 0, 0)),
        pl.BlockSpec((window, head_dim), lambda i, me: (0, 0)),
        pl.BlockSpec((window, head_dim), lambda i, me: (0, 0)),
        pl.BlockSpec((2, window, head_dim), lambda i, me: (0, 0, 0)),
    ]
    out_shape = [
        jax.ShapeDtypeStruct(queries.shape, BF16),
        jax.ShapeDtypeStruct(keys.shape, BF16),
        jax.ShapeDtypeStruct(keys.shape, BF16),
        jax.ShapeDtypeStruct((window, head_dim), F32),
        jax.ShapeDtypeStruct((window, head_dim), F32),
        jax.ShapeDtypeStruct((2, window, head_dim), BF16),
    ]
    pairs = groups * tok_rows * (window + BLOCK)
    return pl.pallas_call(
        functools.partial(head_kernel, head, pieces, len(before)),
        grid_spec=pltpu.PrefetchScalarGridSpec(
            num_scalar_prefetch=1,
            grid=(steps,),
            in_specs=in_specs,
            out_specs=out_specs,
            scratch_shapes=[
                pltpu.VMEM((ext, head_dim), BF16),
                pltpu.VMEM((ext, head_dim), BF16),
                pltpu.VMEM((head_dim, ext), BF16),
                pltpu.VMEM((ext, head_dim), F32),
                pltpu.VMEM((ext, head_dim), F32),
                pltpu.VMEM((window + BLOCK, groups * BLOCK), BF16),
            ],
        ),
        out_shape=out_shape,
        input_output_aliases={n_in + i: i for i in range(len(before))},
        compiler_params=pltpu.CompilerParams(vmem_limit_bytes=40 * 1024 * 1024),
        cost_estimate=pl.CostEstimate(
            flops=10 * pairs * head_dim * 2, bytes_accessed=8 * tok_rows * head_dim * 2, transcendentals=pairs
        ),
        name="head_backward",
    )(me, queries, key_rim, keys, value_rim, values, lse, start, *cotans, *deltas, *before)


def join_kernel(dk_tail_ref, dv_tail_ref, back_ref, dk_in, dv_in, dk_ref, dv_ref):
    dk_ref[0] = (dk_tail_ref[...] + back_ref[0].astype(F32)).astype(BF16)
    dv_ref[0] = (dv_tail_ref[...] + back_ref[1].astype(F32)).astype(BF16)


def join_call(head, dk_tail, dv_tail, back, grad_keys, grad_values):
    window, head_dim = dk_tail.shape
    last = grad_keys.shape[1] // window - 1
    tail = pl.BlockSpec((window, head_dim), lambda i: (0, 0))
    out = pl.BlockSpec((1, window, head_dim), lambda i: (head, last, 0))
    return pl.pallas_call(
        join_kernel,
        grid=(1,),
        in_specs=[
            tail,
            tail,
            pl.BlockSpec((2, window, head_dim), lambda i: (0, 0, 0)),
            pl.BlockSpec(memory_space=pl.ANY),
            pl.BlockSpec(memory_space=pl.ANY),
        ],
        out_specs=[out, out],
        out_shape=[jax.ShapeDtypeStruct(grad_keys.shape, BF16)] * 2,
        input_output_aliases={3: 0, 4: 1},
        name="join_tail",
    )(dk_tail, dv_tail, back, grad_keys, grad_values)


def body(queries, key_states, value_states, attn_output, out_cotangent, logsumexp, doc_start):
    kv_heads, tok_rows, head_dim = key_states.shape
    q_heads = queries.shape[0]
    groups = q_heads // kv_heads
    window = W
    pieces = lax.axis_size("head")
    me = lax.axis_index("head")
    total_heads = out_cotangent.shape[1] // head_dim
    width = q_heads * head_dim
    cols = groups * head_dim

    def sent(block, distance):
        route = [(i, (i + distance) % pieces) for i in range(pieces)]
        return lax.ppermute(block, "head", route)

    cotans = []
    for head in range(kv_heads):
        parts = []
        for k in range(pieces):
            target = lax.rem(me + k, pieces)
            part = lax.dynamic_slice_in_dim(out_cotangent, target * width + head * cols, cols, 1)
            parts.append(part if k == 0 else sent(part, k))
        cotans.append(parts)
    deltas_here = row_deltas(out_cotangent, attn_output, total_heads)
    deltas = []
    for k in range(pieces):
        target = lax.rem(me + k, pieces)
        part = lax.dynamic_slice_in_dim(deltas_here, target * q_heads, q_heads, 0)
        deltas.append(part if k == 0 else sent(part, k))
    key_rim, value_rim = from_behind(
        (key_states[:, tok_rows - window :], value_states[:, tok_rows - window :]), "ctx", 1
    )
    start = doc_start[None, :] - lax.axis_index("ctx") * tok_rows + window
    me_array = me.astype(jnp.int32)[None]

    before = []
    tails = []
    for head in range(kv_heads):
        got = head_call(
            head, me_array, queries, key_rim, key_states, value_rim, value_states,
            logsumexp, start, cotans[head], deltas, before,
        )
        before = list(got[:3])
        tails.append((got[3], got[4], from_behind(got[5], "ctx", -1)))
    grad_queries, grad_keys, grad_values = before
    for head in range(kv_heads):
        grad_keys, grad_values = join_call(head, *tails[head], grad_keys, grad_values)
    return (grad_queries, grad_keys, grad_values)


def solution(mesh):
    return jax.shard_map(
        body,
        mesh=mesh,
        in_specs=(
            P("head", "ctx", None),
            P("head", "ctx", None),
            P("head", "ctx", None),
            P(("ctx", "head"), None),
            P(("ctx", "head"), None),
            P("head", "ctx"),
            P("ctx"),
        ),
        out_specs=(P("head", "ctx", None), P("head", "ctx", None), P("head", "ctx", None)),
        check_vma=False,
    )
```

time: 553 us -> 247 us (0.45)
  matrix products: 247 us -> 0 us
  waiting for transfers between devices: 196 us -> 15 us
  Pallas kernels: 0 us -> 156 us
  local copies, waits for them, and re-layouts: 55.4 us -> 20.7 us
  other arithmetic: 29.6 us -> 0.7 us
  starting transfers between devices: 22.2 us -> 50.7 us
    dot_general x20 -> x0, matrix products: 247 us -> none  [the longest x4 60.1 us: band_tile(): jnp.einsum('rkgd,kjd->kgrj', cotan_block, value_block, preferred_element_...]
    pallas_call x0 -> x9, Pallas kernels: none -> 156 us  [the longest x4 141 us: head_call(): pl.pallas_call(functools.partial(head_kernel, head, pieces, len(before)),...]
    all_to_all x2 -> x0, waiting for transfers between devices: 141 us -> none  [the longest x1 79.9 us: body(): lax.all_to_all(seq_output, 'head', split_axis=1, concat_axis=0, tiled=True)]
    ppermute x4 -> x6, waiting for transfers between devices: 55.3 us -> 1.38 us  [from_behind(): return lax.ppermute(block, axis, route)]
    ppermute x0 -> x15, starting transfers between devices: none -> 31.2 us  [sent(): return lax.ppermute(block, 'head', route)]
    ppermute x0 -> x15, waiting for transfers between devices: none -> 13.7 us  [sent(): return lax.ppermute(block, 'head', route)]
    reshape x4 -> x0, local copies, waits for them, and re-layouts: 13 us -> none  [the longest x1 6.47 us: body(): out_cotangent.reshape(out_cotangent.shape[0], total_heads, head_dim)]
    all_to_all x2 -> x0, starting transfers between devices: 10.3 us -> none  [the longest x1 5.42 us: body(): lax.all_to_all(seq_output, 'head', split_axis=1, concat_axis=0, tiled=True)]
  transfers between devices with their start and end apart: 6 -> 21, of which waited for: 6 -> 4; matrix products, arithmetic and copies ran while one was open for 5% -> 3% of each run, Pallas kernels for 0% -> 63%
where the time goes in v1:
time: 247 us; the launch traced here: 244 us
  Pallas kernels  156 us (63%)
  starting transfers between devices  50.7 us (21%)
  local copies, waits for them, and re-layouts  20.7 us (8%)
  waiting for transfers between devices  15 us (6%)
    pallas_call x4, Pallas kernels, head_call(): pl.pallas_call(functools.partial(head_kernel, head, pieces, len(before)),...  141 us
    ppermute x15, starting transfers between devices, sent(): return lax.ppermute(block, 'head', route)  31.2 us
    ppermute x6, starting transfers between devices, from_behind(): return lax.ppermute(block, axis, route)  19.5 us
    ppermute x15, waiting for transfers between devices, sent(): return lax.ppermute(block, 'head', route)  13.7 us
    unnamed x36, local copies, waits for them, and re-layouts  11.9 us
    pallas_call x4, Pallas kernels, join_call(): pl.pallas_call(join_kernel, grid=(1,), in_specs=[tail, tail, pl.BlockSpec...  8.77 us
    pallas_call x1, Pallas kernels, row_deltas(): pl.pallas_call(delta_kernel, grid=(rows // step,), in_specs=[pl.BlockSpec...  6.25 us
  transfers between devices with their start and end apart: 21, of which 4 were waited for; matrix products, arithmetic and copies ran while one was open for 3% of the time, Pallas kernels for 63%

profile of v1, /device:TPU:1, one launch (start us, length us, event | category | flops | bytes accessed | tf_op | source)
XLA Modules:
  0.0 244.3 jit_solution(16715697108820560770)
XLA Ops:
  0.6 2.4 slice.7
  3.1 4.5 %collective-permute-start.1 = (bf16[4,1024,128]{2,1,0:T(8,128)(2,1)}, bf16[4,1024,128]{2,1,0:T(8,128)(2,1)}, u32[]{:S(2)}, u32[]{:S(2)}) collective-permute-start(bf16[4,1024,128]{2,1,0:T(8,128)(2,1)} %slice.7), channel_id=1, source_target_pairs={{0,4},{4,8},{8,12},{12,16},{16,20},{20,24},{24,28},{1,5},{5,9},{9,... | collective-permute-start | bytes 3145736 | tf_op jit(solution)/shard_map/ppermute | solution.py:24
  10.6 6.3 %row_deltas.1 = f32[32,512]{1,0:T(8,128)} custom-call(bf16[512,4096]{1,0:T(8,128)(2,1)} %cotan_ref.1, bf16[512,4096]{1,0:T(8,128)(2,1)} %output_ref.1), custom_call_target="tpu_custom_call" | custom-call | flops 268435456 | bytes 8388608 | tf_op jit(solution)/shard_map/row_deltas/pallas_call | solution.py:42
  18.2 3.3 %collective-permute-start.7 = (f32[8,512]{1,0:T(8,128)S(1)}, f32[8,512]{1,0:T(8,128)S(1)}, u32[]{:S(2)}, u32[]{:S(2)}) collective-permute-start(f32[8,512]{1,0:T(8,128)S(1)} %get-tuple-element.83), channel_id=1, source_target_pairs={{0,3},{1,0},{2,1},{3,2},{4,7},{5,4},{6,5},{7,6},{8,11},{9,8},{10,9... | collective-permute-start | bytes 49160 | tf_op jit(solution)/shard_map/ppermute | solution.py:245
  22.0 3.9 %constant_dynamic-slice_fusion = (bf16[512,256]{1,0:T(8,128)(2,1)}, bf16[512,256]{1,0:T(8,128)(2,1)}, bf16[512,256]{1,0:T(8,128)(2,1)S(1)}, bf16[512,256]{1,0:T(...) fusion(bf16[512,4096]{1,0:T(8,128)(2,1)} %cotan_ref.1, ...), kind=kLoop, calls=%fused_computation.1 | loop fusion | bytes 8388672 | tf_op jit(solution)/shard_map/dynamic_slice | solution.py:252
  25.9 2.9 %collective-permute-start.16 = (bf16[512,256]{1,0:T(8,128)(2,1)}, bf16[512,256]{1,0:T(8,128)(2,1)S(1)}, u32[]{:S(2)}, u32[]{:S(2)}) collective-permute-start(bf16[512,256]{1,0:T(8,128)(2,1)} %get-tuple-element.67), channel_id=1, source_target_pairs={{0,3},{1,0},{2,1},{3,2},{4,7},{5,4},{6,5},{7,6},{8,11},{9,8},{10,9... | collective-permute-start | bytes 786440 | tf_op jit(solution)/shard_map/ppermute | solution.py:245
  30.1 2.6 %collective-permute-done.16.refs_10_ = bf16[512,256]{1,0:T(8,128)(2,1)S(1)} collective-permute-done((bf16[512,256]{1,0:T(8,128)(2,1)}, bf16[512,256]{1,0:T(8,128)(2,1)S(1)}, u32[]{:S(2)}, u32[]{:S(2)}) %collective-permute-start.16) | collective-permute-done | bytes 262176 | tf_op jit(solution)/shard_map/ppermute | solution.py:245
  32.7 3.9 %collective-permute-start.13 = (bf16[512,256]{1,0:T(8,128)(2,1)}, bf16[512,256]{1,0:T(8,128)(2,1)S(1)}, u32[]{:S(2)}, u32[]{:S(2)}) collective-permute-start(bf16[512,256]{1,0:T(8,128)(2,1)} %get-tuple-element.70), channel_id=1, source_target_pairs={{0,3},{1,0},{2,1},{3,2},{4,7},{5,4},{6,5},{7,6},{8,11},{9,8},{10,9... | collective-permute-start | bytes 786440 | tf_op jit(solution)/shard_map/ppermute | solution.py:245
  36.6 2.6 %collective-permute-done.14.refs_8_ = bf16[512,256]{1,0:T(8,128)(2,1)} collective-permute-done((bf16[512,256]{1,0:T(8,128)(2,1)}, bf16[512,256]{1,0:T(8,128)(2,1)}, u32[]{:S(2)}, u32[]{:S(2)}) %collective-permute-start.14) | collective-permute-done | bytes 262176 | tf_op jit(solution)/shard_map/ppermute | solution.py:245
  39.3 5.4 %collective-permute-start.12 = (bf16[512,256]{1,0:T(8,128)(2,1)}, bf16[512,256]{1,0:T(8,128)(2,1)S(1)}, u32[]{:S(2)}, u32[]{:S(2)}) collective-permute-start(bf16[512,256]{1,0:T(8,128)(2,1)} %get-tuple-element.71), channel_id=1, source_target_pairs={{0,2},{1,3},{2,0},{3,1},{4,6},{5,7},{6,4},{7,5},{8,10},{9,11},{10,... | collective-permute-start | bytes 786440 | tf_op jit(solution)/shard_map/ppermute | solution.py:245
  44.7 8.3 %collective-permute-done.15.refs_9_ = bf16[512,256]{1,0:T(8,128)(2,1)} collective-permute-done((bf16[512,256]{1,0:T(8,128)(2,1)}, bf16[512,256]{1,0:T(8,128)(2,1)}, u32[]{:S(2)}, u32[]{:S(2)}) %collective-permute-start.15) | collective-permute-done | bytes 262176 | tf_op jit(solution)/shard_map/ppermute | solution.py:245
  53.0 7.8 %collective-permute-start.11 = (bf16[512,256]{1,0:T(8,128)(2,1)}, bf16[512,256]{1,0:T(8,128)(2,1)S(1)}, u32[]{:S(2)}, u32[]{:S(2)}) collective-permute-start(bf16[512,256]{1,0:T(8,128)(2,1)} %get-tuple-element.72), channel_id=1, source_target_pairs={{0,1},{1,2},{2,3},{3,0},{4,5},{5,6},{6,7},{7,4},{8,9},{9,10},{10,1... | collective-permute-start | bytes 786440 | tf_op jit(solution)/shard_map/ppermute | solution.py:245
  60.8 2.8 %collective-permute-start.10 = (bf16[512,256]{1,0:T(8,128)(2,1)}, bf16[512,256]{1,0:T(8,128)(2,1)S(1)}, u32[]{:S(2)}, u32[]{:S(2)}) collective-permute-start(bf16[512,256]{1,0:T(8,128)(2,1)} %get-tuple-element.74), channel_id=1, source_target_pairs={{0,3},{1,0},{2,1},{3,2},{4,7},{5,4},{6,5},{7,6},{8,11},{9,8},{10,9... | collective-permute-start | bytes 786440 | tf_op jit(solution)/shard_map/ppermute | solution.py:245
  65.6 2.2 copy-done.10
  67.8 35.4 %head_backward.4 = (bf16[8,2048,128]{2,1,0:T(8,128)(2,1)}, bf16[4,2048,128]{2,1,0:T(8,128)(2,1)}, bf16[4,2048,128]{2,1,0:T(8,128)(2,1)}, f32[1024,128]{1,0:T(8,1...) custom-call(s32[1]{0:T(128)} %bitcast.me_ref, bf16[8,2048,128]{2,1,0:T(8,128)(2,1)S(1)} %copy-done.10, ...), custom_call_target="tpu_custom_call" | custom-call | flops 12079595520 | bytes 4194304 | tf_op jit(solution)/shard_map/head_backward/pallas_call | solution.py:179
  108.3 35.4 %head_backward.5 = (bf16[8,2048,128]{2,1,0:T(8,128)(2,1)}, bf16[4,2048,128]{2,1,0:T(8,128)(2,1)}, bf16[4,2048,128]{2,1,0:T(8,128)(2,1)}, f32[1024,128]{1,0:T(8,1...) custom-call(s32[1]{0:T(128)} %bitcast.me_ref, ...), custom_call_target="tpu_custom_call", output_to_operand_aliasing={{0}: (16, {}), {1}: (17, {}), {2}: (18, {})} | custom-call | flops 12079595520 | bytes 4194304 | tf_op jit(solution)/shard_map/head_backward/pallas_call | solution.py:179
  145.5 35.2 %head_backward.6 = (bf16[8,2048,128]{2,1,0:T(8,128)(2,1)}, bf16[4,2048,128]{2,1,0:T(8,128)(2,1)}, bf16[4,2048,128]{2,1,0:T(8,128)(2,1)}, f32[1024,128]{1,0:T(8,1...) custom-call(s32[1]{0:T(128)} %bitcast.me_ref, ...), custom_call_target="tpu_custom_call", output_to_operand_aliasing={{0}: (16, {}), {1}: (17, {}), {2}: (18, {})} | custom-call | flops 12079595520 | bytes 4194304 | tf_op jit(solution)/shard_map/head_backward/pallas_call | solution.py:179
  182.3 7.3 %collective-permute-start.18 = (bf16[2,1024,128]{2,1,0:T(8,128)(2,1)S(1)}, bf16[2,1024,128]{2,1,0:T(8,128)(2,1)}, u32[]{:S(2)}, u32[]{:S(2)}) collective-permute-start(bf16[2,1024,128]{2,1,0:T(8,128)(2,1)S(1)} %get-tuple-element.50), channel_id=1, source_target_pairs={{4,0},{8,4},{12,8},{16,12},{20,16},{24,20},{28,24},{5,1},{9,5},{13... | collective-permute-start | bytes 1572872 | tf_op jit(solution)/shard_map/ppermute | solution.py:24
  189.7 1.9 collective-permute-start.19
  193.5 35.4 %head_backward.7 = (bf16[8,2048,128]{2,1,0:T(8,128)(2,1)}, bf16[4,2048,128]{2,1,0:T(8,128)(2,1)}, bf16[4,2048,128]{2,1,0:T(8,128)(2,1)}, f32[1024,128]{1,0:T(8,1...) custom-call(s32[1]{0:T(128)} %bitcast.me_ref, ...), custom_call_target="tpu_custom_call", output_to_operand_aliasing={{0}: (16, {}), {1}: (17, {}), {2}: (18, {})} | custom-call | flops 12079595520 | bytes 4194304 | tf_op jit(solution)/shard_map/head_backward/pallas_call | solution.py:179
  233.3 2.2 join_tail.4
  235.5 2.2 join_tail.5
  237.7 2.2 join_tail.6
  242.1 2.2 join_tail.7
  (68 shorter events, 25.1 us)
Async XLA Ops:
  3.1 57.8 %collective-permute-start.1 = (bf16[4,1024,128]{2,1,0:T(8,128)(2,1)}, bf16[4,1024,128]{2,1,0:T(8,128)(2,1)}, u32[]{:S(2)}, u32[]{:S(2)}) collective-permute-start(bf16[4,1024,128]{2,1,0:T(8,128)(2,1)} %slice.7), channel_id=1, source_target_pairs={{0,4},{4,8},{8,12},{12,16},{16,20},{20,24},{24,28},{1,5},{5,9},{9,... | collective-permute-start | bytes 3145736 | tf_op jit(solution)/shard_map/ppermute | solution.py:24
  8.6 55.0 %collective-permute-start = (bf16[4,1024,128]{2,1,0:T(8,128)(2,1)}, bf16[4,1024,128]{2,1,0:T(8,128)(2,1)}, u32[]{:S(2)}, u32[]{:S(2)}) collective-permute-start(bf16[4,1024,128]{2,1,0:T(8,128)(2,1)} %slice.6), channel_id=1, source_target_pairs={{0,4},{4,8},{8,12},{12,16},{16,20},{20,24},{24,28},{1,5},{5,9},{9,... | collective-permute-start | bytes 3145736 | tf_op jit(solution)/shard_map/ppermute | solution.py:24
  18.2 7.7 %collective-permute-start.7 = (f32[8,512]{1,0:T(8,128)S(1)}, f32[8,512]{1,0:T(8,128)S(1)}, u32[]{:S(2)}, u32[]{:S(2)}) collective-permute-start(f32[8,512]{1,0:T(8,128)S(1)} %get-tuple-element.83), channel_id=1, source_target_pairs={{0,3},{1,0},{2,1},{3,2},{4,7},{5,4},{6,5},{7,6},{8,11},{9,8},{10,9... | collective-permute-start | bytes 49160 | tf_op jit(solution)/shard_map/ppermute | solution.py:245
  21.5 7.2 %collective-permute-start.6 = (f32[8,512]{1,0:T(8,128)}, f32[8,512]{1,0:T(8,128)S(1)}, u32[]{:S(2)}, u32[]{:S(2)}) collective-permute-start(f32[8,512]{1,0:T(8,128)} %get-tuple-element.84), channel_id=1, source_target_pairs={{0,2},{1,3},{2,0},{3,1},{4,6},{5,7},{6,4},{7,5},{8,10},{9,11},{10,... | collective-permute-start | bytes 49160 | tf_op jit(solution)/shard_map/ppermute | solution.py:245
  21.5 7.2 %collective-permute-start.5 = (f32[8,512]{1,0:T(8,128)S(1)}, f32[8,512]{1,0:T(8,128)S(1)}, u32[]{:S(2)}, u32[]{:S(2)}) collective-permute-start(f32[8,512]{1,0:T(8,128)S(1)} %get-tuple-element.85), channel_id=1, source_target_pairs={{0,1},{1,2},{2,3},{3,0},{4,5},{5,6},{6,7},{7,4},{8,9},{9,10},{10,1... | collective-permute-start | bytes 49160 | tf_op jit(solution)/shard_map/ppermute | solution.py:245
  22.0 42.0 %copy-start.11 = (f32[8,2048]{1,0:T(8,128)S(1)}, f32[8,2048]{1,0:T(8,128)}, u32[]{:S(2)}) copy-start(f32[8,2048]{1,0:T(8,128)} %refs_5_.7) | copy-start | bytes 196612
  25.9 6.9 %collective-permute-start.16 = (bf16[512,256]{1,0:T(8,128)(2,1)}, bf16[512,256]{1,0:T(8,128)(2,1)S(1)}, u32[]{:S(2)}, u32[]{:S(2)}) collective-permute-start(bf16[512,256]{1,0:T(8,128)(2,1)} %get-tuple-element.67), channel_id=1, source_target_pairs={{0,3},{1,0},{2,1},{3,2},{4,7},{5,4},{6,5},{7,6},{8,11},{9,8},{10,9... | collective-permute-start | bytes 786440 | tf_op jit(solution)/shard_map/ppermute | solution.py:245
  28.8 10.5 %collective-permute-start.14 = (bf16[512,256]{1,0:T(8,128)(2,1)}, bf16[512,256]{1,0:T(8,128)(2,1)}, u32[]{:S(2)}, u32[]{:S(2)}) collective-permute-start(bf16[512,256]{1,0:T(8,128)(2,1)} %get-tuple-element.68), channel_id=1, source_target_pairs={{0,1},{1,2},{2,3},{3,0},{4,5},{5,6},{6,7},{7,4},{8,9},{9,10},{10,1... | collective-permute-start | bytes 786440 | tf_op jit(solution)/shard_map/ppermute | solution.py:245
  28.8 24.3 %collective-permute-start.15 = (bf16[512,256]{1,0:T(8,128)(2,1)}, bf16[512,256]{1,0:T(8,128)(2,1)}, u32[]{:S(2)}, u32[]{:S(2)}) collective-permute-start(bf16[512,256]{1,0:T(8,128)(2,1)} %get-tuple-element.82), channel_id=1, source_target_pairs={{0,2},{1,3},{2,0},{3,1},{4,6},{5,7},{6,4},{7,5},{8,10},{9,11},{10,... | collective-permute-start | bytes 786440 | tf_op jit(solution)/shard_map/ppermute | solution.py:245
  32.7 72.0 %collective-permute-start.13 = (bf16[512,256]{1,0:T(8,128)(2,1)}, bf16[512,256]{1,0:T(8,128)(2,1)S(1)}, u32[]{:S(2)}, u32[]{:S(2)}) collective-permute-start(bf16[512,256]{1,0:T(8,128)(2,1)} %get-tuple-element.70), channel_id=1, source_target_pairs={{0,3},{1,0},{2,1},{3,2},{4,7},{5,4},{6,5},{7,6},{8,11},{9,8},{10,9... | collective-permute-start | bytes 786440 | tf_op jit(solution)/shard_map/ppermute | solution.py:245
  39.3 66.9 %collective-permute-start.12 = (bf16[512,256]{1,0:T(8,128)(2,1)}, bf16[512,256]{1,0:T(8,128)(2,1)S(1)}, u32[]{:S(2)}, u32[]{:S(2)}) collective-permute-start(bf16[512,256]{1,0:T(8,128)(2,1)} %get-tuple-element.71), channel_id=1, source_target_pairs={{0,2},{1,3},{2,0},{3,1},{4,6},{5,7},{6,4},{7,5},{8,10},{9,11},{10,... | collective-permute-start | bytes 786440 | tf_op jit(solution)/shard_map/ppermute | solution.py:245
  53.0 55.0 %collective-permute-start.11 = (bf16[512,256]{1,0:T(8,128)(2,1)}, bf16[512,256]{1,0:T(8,128)(2,1)S(1)}, u32[]{:S(2)}, u32[]{:S(2)}) collective-permute-start(bf16[512,256]{1,0:T(8,128)(2,1)} %get-tuple-element.72), channel_id=1, source_target_pairs={{0,1},{1,2},{2,3},{3,0},{4,5},{5,6},{6,7},{7,4},{8,9},{9,10},{10,1... | collective-permute-start | bytes 786440 | tf_op jit(solution)/shard_map/ppermute | solution.py:245
  60.8 84.5 %collective-permute-start.10 = (bf16[512,256]{1,0:T(8,128)(2,1)}, bf16[512,256]{1,0:T(8,128)(2,1)S(1)}, u32[]{:S(2)}, u32[]{:S(2)}) collective-permute-start(bf16[512,256]{1,0:T(8,128)(2,1)} %get-tuple-element.74), channel_id=1, source_target_pairs={{0,3},{1,0},{2,1},{3,2},{4,7},{5,4},{6,5},{7,6},{8,11},{9,8},{10,9... | collective-permute-start | bytes 786440 | tf_op jit(solution)/shard_map/ppermute | solution.py:245
  63.7 81.8 %collective-permute-start.9 = (bf16[512,256]{1,0:T(8,128)(2,1)}, bf16[512,256]{1,0:T(8,128)(2,1)S(1)}, u32[]{:S(2)}, u32[]{:S(2)}) collective-permute-start(bf16[512,256]{1,0:T(8,128)(2,1)} %get-tuple-element.75), channel_id=1, source_target_pairs={{0,2},{1,3},{2,0},{3,1},{4,6},{5,7},{6,4},{7,5},{8,10},{9,11},{10,... | collective-permute-start | bytes 786440 | tf_op jit(solution)/shard_map/ppermute | solution.py:245
  67.8 38.4 %copy-start.16 = (bf16[512,256]{1,0:T(8,128)(2,1)S(1)}, bf16[512,256]{1,0:T(8,128)(2,1)}, u32[]{:S(2)}) copy-start(bf16[512,256]{1,0:T(8,128)(2,1)} %get-tuple-element.78) | copy-start | bytes 786436
  67.8 40.3 %copy-start.15 = (bf16[512,256]{1,0:T(8,128)(2,1)S(1)}, bf16[512,256]{1,0:T(8,128)(2,1)}, u32[]{:S(2)}) copy-start(bf16[512,256]{1,0:T(8,128)(2,1)} %get-tuple-element.79) | copy-start | bytes 786436
  104.8 40.7 %collective-permute-start.8 = (bf16[512,256]{1,0:T(8,128)(2,1)S(1)}, bf16[512,256]{1,0:T(8,128)(2,1)S(1)}, u32[]{:S(2)}, u32[]{:S(2)}) collective-permute-start(bf16[512,256]{1,0:T(8,128)(2,1)S(1)} %copy-done.17), channel_id=1, source_target_pairs={{0,1},{1,2},{2,3},{3,0},{4,5},{5,6},{6,7},{7,4},{8,9},{9,10},{10,1... | collective-permute-start | bytes 786440 | tf_op jit(solution)/shard_map/ppermute | solution.py:245
  106.2 85.4 %collective-permute-start.4 = (bf16[512,256]{1,0:T(8,128)(2,1)S(1)}, bf16[512,256]{1,0:T(8,128)(2,1)S(1)}, u32[]{:S(2)}, u32[]{:S(2)}) collective-permute-start(bf16[512,256]{1,0:T(8,128)(2,1)S(1)} %copy-done.16), channel_id=1, source_target_pairs={{0,3},{1,0},{2,1},{3,2},{4,7},{5,4},{6,5},{7,6},{8,11},{9,8},{10,9... | collective-permute-start | bytes 786440 | tf_op jit(solution)/shard_map/ppermute | solution.py:245
  108.1 85.4 %collective-permute-start.3 = (bf16[512,256]{1,0:T(8,128)(2,1)S(1)}, bf16[512,256]{1,0:T(8,128)(2,1)S(1)}, u32[]{:S(2)}, u32[]{:S(2)}) collective-permute-start(bf16[512,256]{1,0:T(8,128)(2,1)S(1)} %copy-done.15), channel_id=1, source_target_pairs={{0,2},{1,3},{2,0},{3,1},{4,6},{5,7},{6,4},{7,5},{8,10},{9,11},{10,... | collective-permute-start | bytes 786440 | tf_op jit(solution)/shard_map/ppermute | solution.py:245
  145.3 48.2 %collective-permute-start.2 = (bf16[512,256]{1,0:T(8,128)(2,1)S(1)}, bf16[512,256]{1,0:T(8,128)(2,1)S(1)}, u32[]{:S(2)}, u32[]{:S(2)}) collective-permute-start(bf16[512,256]{1,0:T(8,128)(2,1)S(1)} %copy-done.14), channel_id=1, source_target_pairs={{0,1},{1,2},{2,3},{3,0},{4,5},{5,6},{6,7},{7,4},{8,9},{9,10},{10,1... | collective-permute-start | bytes 786440 | tf_op jit(solution)/shard_map/ppermute | solution.py:245
  182.3 55.4 %collective-permute-start.18 = (bf16[2,1024,128]{2,1,0:T(8,128)(2,1)S(1)}, bf16[2,1024,128]{2,1,0:T(8,128)(2,1)}, u32[]{:S(2)}, u32[]{:S(2)}) collective-permute-start(bf16[2,1024,128]{2,1,0:T(8,128)(2,1)S(1)} %get-tuple-element.50), channel_id=1, source_target_pairs={{4,0},{8,4},{12,8},{16,12},{20,16},{24,20},{28,24},{5,1},{9,5},{13... | collective-permute-start | bytes 1572872 | tf_op jit(solution)/shard_map/ppermute | solution.py:24
  189.7 45.9 %collective-permute-start.19 = (bf16[2,1024,128]{2,1,0:T(8,128)(2,1)}, bf16[2,1024,128]{2,1,0:T(8,128)(2,1)}, u32[]{:S(2)}, u32[]{:S(2)}) collective-permute-start(bf16[2,1024,128]{2,1,0:T(8,128)(2,1)} %get-tuple-element.53), channel_id=1, source_target_pairs={{4,0},{8,4},{12,8},{16,12},{20,16},{24,20},{28,24},{5,1},{9,5},{13... | collective-permute-start | bytes 1572872 | tf_op jit(solution)/shard_map/ppermute | solution.py:24
  191.6 40.9 %collective-permute-start.20 = (bf16[2,1024,128]{2,1,0:T(8,128)(2,1)S(1)}, bf16[2,1024,128]{2,1,0:T(8,128)(2,1)S(1)}, u32[]{:S(2)}, u32[]{:S(2)}) collective-permute-start(bf16[2,1024,128]{2,1,0:T(8,128)(2,1)S(1)} %get-tuple-element.56), channel_id=1, source_target_pairs={{4,0},{8,4},{12,8},{16,12},{20,16},{24,20},{28,24},{5,1},{9,5},{13... | collective-permute-start | bytes 1572872 | tf_op jit(solution)/shard_map/ppermute | solution.py:24
  230.6 10.7 %collective-permute-start.17 = (bf16[2,1024,128]{2,1,0:T(8,128)(2,1)}, bf16[2,1024,128]{2,1,0:T(8,128)(2,1)S(1)}, u32[]{:S(2)}, u32[]{:S(2)}) collective-permute-start(bf16[2,1024,128]{2,1,0:T(8,128)(2,1)} %get-tuple-element.47), channel_id=1, source_target_pairs={{4,0},{8,4},{12,8},{16,12},{20,16},{24,20},{28,24},{5,1},{9,5},{13... | collective-permute-start | bytes 1572872 | tf_op jit(solution)/shard_map/ppermute | solution.py:24
  (15 other events, 92.9 us)

commit v2 on v1

v2 whole, which is shorter than its diff:
```python
import functools
import math

import jax
import jax.numpy as jnp
from jax import lax
from jax.experimental import pallas as pl
from jax.experimental.pallas import tpu as pltpu
from jax.sharding import PartitionSpec as P

W = 1024
QPRE = 168
BLOCK = 128
SUB = 32
UNROLL = 4
VMEM_LIMIT = 56 * 1024 * 1024
LOG2E = math.log2(math.e)
F32 = jnp.float32
BF16 = jnp.bfloat16
NT = (((1,), (1,)), ((), ()))
NN = (((1,), (0,)), ((), ()))


def from_behind(block, axis, distance):
    devices = range(lax.axis_size(axis))
    route = [(i - distance, i) for i in devices if i - distance in devices]
    return lax.ppermute(block, axis, route)


def pack_kernel(pieces, me_ref, *refs):
    cotan_refs, output_refs = refs[:pieces], refs[pieces : 2 * pieces]
    out_refs, rows_ref = refs[2 * pieces + 1 : 3 * pieces + 1], refs[3 * pieces + 1]
    rows, cols = cotan_refs[0].shape
    groups = cols // BLOCK
    in_piece = rows // BLOCK
    head_of = lax.broadcasted_iota(jnp.int32, (16, cols), 1) // BLOCK
    member = (head_of == lax.broadcasted_iota(jnp.int32, (16, cols), 0)).astype(BF16)
    rows_ref[...] = jnp.zeros_like(rows_ref)
    for k in range(pieces):
        cotan = cotan_refs[k][...]
        product = cotan.astype(F32) * output_refs[k][...].astype(F32)
        high = product.astype(BF16)
        low = (product - high.astype(F32)).astype(BF16)
        delta = lax.dot_general(member, high, NT, preferred_element_type=F32)
        delta = delta + lax.dot_general(member, low, NT, preferred_element_type=F32)
        out_refs[k][:rows] = cotan
        for part in range(3):
            rounded = delta.astype(BF16).astype(F32)
            delta = delta - rounded
            for j in range(in_piece):
                for i in range(groups):
                    rows_ref[
                        part * in_piece + j : part * in_piece + j + 1, i * BLOCK : (i + 1) * BLOCK
                    ] = rounded[i : i + 1, j * BLOCK : (j + 1) * BLOCK]
        out_refs[k][rows:] = rows_ref[...].astype(BF16)


def pack_call(head, me, cotan, output, kv_heads, cols, pieces, after):
    rows = cotan.shape[0]
    assert 3 * (rows // BLOCK) <= 16

    def piece_at(k):
        return pl.BlockSpec(
            (rows, cols), lambda i, me: (0, lax.rem(me[0] + k, pieces) * kv_heads + head)
        )

    in_specs = [piece_at(k) for k in range(pieces)] * 2 + [pl.BlockSpec(memory_space=pl.ANY)]
    operands = [cotan] * pieces + [output] * pieces + [after]
    out_specs = [pl.BlockSpec((rows + 16, cols), lambda i, me: (0, 0))] * pieces
    out_shape = [jax.ShapeDtypeStruct((rows + 16, cols), BF16)] * pieces
    scratch = [pltpu.VMEM((16, cols), F32)]
    return pl.pallas_call(
        functools.partial(pack_kernel, pieces),
        grid_spec=pltpu.PrefetchScalarGridSpec(
            num_scalar_prefetch=1,
            grid=(1,),
            in_specs=in_specs,
            out_specs=out_specs,
            scratch_shapes=scratch,
        ),
        out_shape=out_shape,
        compiler_params=pltpu.CompilerParams(vmem_limit_bytes=VMEM_LIMIT),
        cost_estimate=pl.CostEstimate(
            flops=4 * rows * cols * pieces, bytes_accessed=6 * rows * cols * pieces, transcendentals=0
        ),
        name="pack_cotangent",
    )(me, *operands)


def rim_kernel(key_ref, value_ref, after_ref, out_ref):
    out_ref[0] = key_ref[...]
    out_ref[1] = value_ref[...]


def rim_call(keys, values, after):
    kv_heads, tok_rows, head_dim = keys.shape
    last = pl.BlockSpec((1, W, head_dim), lambda i: (i, tok_rows // W - 1, 0))
    return pl.pallas_call(
        rim_kernel,
        grid=(kv_heads,),
        in_specs=[last, last, pl.BlockSpec(memory_space=pl.ANY)],
        out_specs=pl.BlockSpec((2, 1, W, head_dim), lambda i: (0, i, 0, 0)),
        out_shape=jax.ShapeDtypeStruct((2, kv_heads, W, head_dim), BF16),
        name="rims",
    )(keys, values, after)


def head_kernel(head, blocks, carried, closing, aliased, passed, me_ref, *refs):
    refs = list(refs)
    q_ref, kh_ref, ko_ref, vh_ref, vo_ref, lse_ref, start_ref = refs[:7]
    pieces = len(refs) - 7 - 2 * carried - aliased - 2 * passed - (14 if closing else 9)
    cotan_refs = refs[7 : 7 + pieces]
    refs = refs[7 + pieces :]
    dk_in, dv_in = refs[:2] if carried else (None, None)
    refs = refs[2 * carried + aliased + passed :]
    if closing:
        dq_ref, dk_ref, dv_ref, dk_tail_ref, dv_tail_ref, halo_ref = refs[:6]
        k_all, v_all, kt_all, cotan_all, delta_all, ds_all, dk_all, dv_all = refs[6 + passed :]
    else:
        dq_ref, dk_all, dv_all = refs[:3]
        k_all, v_all, kt_all, cotan_all, delta_all, ds_all = refs[3 + passed :]
    window, head_dim = kh_ref.shape[1:]
    groups, tok_rows = q_ref.shape[:2]
    piece_rows = tok_rows // pieces
    in_piece = piece_rows // BLOCK
    span = window + BLOCK
    cols = groups * BLOCK
    scale = QPRE ** (-0.5)
    me = me_ref[0]

    k_all[:window] = kh_ref[0]
    k_all[window:] = ko_ref[0]
    v_all[:window] = vh_ref[0]
    v_all[window:] = vo_ref[0]
    unit = (
        lax.broadcasted_iota(jnp.int32, (head_dim, head_dim), 0)
        == lax.broadcasted_iota(jnp.int32, (head_dim, head_dim), 1)
    ).astype(BF16)
    kt_all[...] = lax.dot_general(unit, k_all[...], NT, preferred_element_type=F32).astype(BF16)
    if carried:
        dk_all[...] = dk_in[...]
        dv_all[...] = dv_in[...]
    else:
        dk_all[...] = jnp.zeros_like(dk_all)
        dv_all[...] = jnp.zeros_like(dv_all)
    ds_all[...] = jnp.zeros_like(ds_all)
    for i in range(pieces):
        source = lax.rem(me - i + pieces, pieces)
        where = pl.ds(pl.multiple_of(source * piece_rows, piece_rows), piece_rows)
        for j in range(groups):
            cotan_all[j, where, :] = cotan_refs[i][:piece_rows, j * head_dim : (j + 1) * head_dim]
        parts = cotan_refs[i][piece_rows:].astype(F32)
        for j in range(in_piece):
            row = parts[j : j + 1] + parts[in_piece + j : in_piece + j + 1]
            delta_all[source * in_piece + j] = row + parts[2 * in_piece + j : 2 * in_piece + j + 1]

    def write_query(first, slot):
        dq = lax.dot_general(
            kt_all[:, pl.ds(first, span)], ds_all[slot], NN, preferred_element_type=F32
        )
        dq = (dq.T * F32(scale)).astype(BF16)
        into = pl.multiple_of(first - first_block * BLOCK, BLOCK)
        dq_ref[:, pl.ds(into, BLOCK), :] = dq.reshape(groups, BLOCK, head_dim)

    token = lax.broadcasted_iota(jnp.int32, (1, cols), 1) % BLOCK
    place = lax.broadcasted_iota(jnp.int32, (SUB, cols), 0)
    chunks = span // BLOCK
    first_block, count = blocks
    unroll = ds_all.shape[0]

    def load(index):
        first = pl.multiple_of(index * BLOCK, BLOCK)
        here = pl.ds(first, BLOCK)
        query = q_ref[:, here, :].reshape(cols, head_dim)
        cotan = cotan_all[:, here, :].reshape(cols, head_dim)

        rows = [lse_ref[head * groups + i : head * groups + i + 1, here] for i in range(groups)]
        lse = jnp.concatenate(rows, axis=1) * F32(LOG2E)
        delta = delta_all[index]
        start = jnp.concatenate([start_ref[:, here]] * groups, axis=1) - first
        lower = jnp.maximum(start, token + 1)
        return first, query, cotan, lse, delta, lower

    def span_of(first, i):
        return pl.ds(pl.multiple_of(first + i * BLOCK, BLOCK), BLOCK)

    def front(block, i):
        first, query, cotan = block[:3]
        rows = span_of(first, i)
        return (
            lax.dot_general(k_all[rows, :], query, NT, preferred_element_type=F32),
            lax.dot_general(v_all[rows, :], cotan, NT, preferred_element_type=F32),
        )

    def back(block, i, probs_low, dscores):
        first, query, cotan = block[:3]
        rows = span_of(first, i)
        dv_all[rows, :] += lax.dot_general(probs_low, cotan, NN, preferred_element_type=F32)
        dk_all[rows, :] += lax.dot_general(dscores, query, NN, preferred_element_type=F32)

    def middle(block, slot, i, scores, dprobs):
        _, _, _, lse, delta, lower = block
        lows = []
        for at in range(0, BLOCK, SUB):
            part = slice(at, at + SUB)
            shift = i * BLOCK + at
            allowed = place >= lower - shift
            if shift + SUB > window:
                allowed = allowed & (place <= token + (window - shift))
            probs = jnp.where(
                allowed, jnp.exp2(scores[part] * F32(scale * LOG2E) - lse), F32(0.0)
            )
            dscores = (probs * (dprobs[part] - delta)).astype(BF16)
            ds_all[slot, shift : shift + SUB, :] = dscores
            lows.append((probs.astype(BF16), dscores))
        probs_low = jnp.concatenate([x for x, _ in lows], axis=0)
        dscores = jnp.concatenate([x for _, x in lows], axis=0)
        return probs_low, dscores

    def some_blocks(index, nothing):
        blocks = [load(first_block + unroll * index + j) for j in range(unroll)]
        stages = [(j, i) for j in range(unroll) for i in range(chunks)]
        ready = front(blocks[0], 0)
        before = first_block + jnp.maximum(unroll * index - 1, 0)
        write_query(pl.multiple_of(before * BLOCK, BLOCK), unroll - 1)
        held = None
        for n, (j, i) in enumerate(stages):
            scores, dprobs = ready
            if n + 1 < len(stages):
                jj, ii = stages[n + 1]
                ready = front(blocks[jj], ii)
            if held is not None:
                back(*held)
            if i == 1 and j > 0:
                write_query(blocks[j - 1][0], j - 1)
            held = (blocks[j], i, *middle(blocks[j], j, i, scores, dprobs))
        back(*held)
        return nothing

    lax.fori_loop(0, count // unroll, some_blocks, 0)
    write_query((first_block + count - 1) * BLOCK, unroll - 1)

    if closing:
        own = dk_ref.shape[1]
        halo_ref[0] = (dk_all[:window] * F32(scale)).astype(BF16)
        halo_ref[1] = dv_all[:window].astype(BF16)
        dk_ref[0] = (dk_all[window : window + own] * F32(scale)).astype(BF16)
        dv_ref[0] = dv_all[window : window + own].astype(BF16)
        dk_tail_ref[...] = dk_all[window + own :] * F32(scale)
        dv_tail_ref[...] = dv_all[window + own :]


def head_call(
    head, blocks, me, queries, rims, keys, values, lse, start, cotans, before, carry, closing, passing
):
    kv_heads, tok_rows, head_dim = keys.shape
    q_heads = queries.shape[0]
    groups = q_heads // kv_heads
    window = rims.shape[2]
    pieces = len(cotans)
    own = tok_rows - window
    ext = tok_rows + window

    def at_head(*block):
        return pl.BlockSpec(block, lambda i, me: (head, 0, 0))

    def full(*block):
        return pl.BlockSpec(block, lambda i, me: (0,) * len(block))

    in_specs = [
        at_head(groups, tok_rows, head_dim),
        pl.BlockSpec((None, 1, window, head_dim), lambda i, me: (0, head, 0, 0)),
        at_head(1, tok_rows, head_dim),
        pl.BlockSpec((None, 1, window, head_dim), lambda i, me: (1, head, 0, 0)),
        at_head(1, tok_rows, head_dim),
        full(q_heads, tok_rows),
        full(1, tok_rows),
    ]
    in_specs += [full(*cotans[0].shape)] * pieces
    in_specs += [full(ext, head_dim)] * len(carry)
    in_specs += [pl.BlockSpec(memory_space=pl.ANY)] * (len(before) + len(passing))
    n_in = 1 + 7 + pieces + len(carry)
    first_block, count = blocks
    unroll = math.gcd(UNROLL, count)
    assert first_block % count == 0
    out_specs = [
        pl.BlockSpec((groups, count * BLOCK, head_dim), lambda i, me: (head, first_block // count, 0))
    ]
    out_shape = [jax.ShapeDtypeStruct(queries.shape, BF16)]
    scratch = [
        pltpu.VMEM((ext, head_dim), BF16),
        pltpu.VMEM((ext, head_dim), BF16),
        pltpu.VMEM((head_dim, ext), BF16),
        pltpu.VMEM((groups, tok_rows, head_dim), BF16),
        pltpu.VMEM((tok_rows // BLOCK, 1, groups * BLOCK), F32),
        pltpu.VMEM((unroll, window + BLOCK, groups * BLOCK), BF16),
    ]
    if closing:
        out_specs += [at_head(1, own, head_dim)] * 2 + [full(window, head_dim)] * 2
        out_specs += [full(2, window, head_dim)]
        out_shape += [jax.ShapeDtypeStruct(keys.shape, BF16)] * 2
        out_shape += [jax.ShapeDtypeStruct((window, head_dim), F32)] * 2
        out_shape += [jax.ShapeDtypeStruct((2, window, head_dim), BF16)]
        scratch += [pltpu.VMEM((ext, head_dim), F32)] * 2
    else:
        out_specs += [full(ext, head_dim)] * 2
        out_shape += [jax.ShapeDtypeStruct((ext, head_dim), F32)] * 2
    aliases = {n_in + i: i for i in range(len(before))}
    for i, array in enumerate(passing):
        aliases[n_in + len(before) + i] = len(out_shape)
        out_shape.append(jax.ShapeDtypeStruct(array.shape, array.dtype))
        out_specs.append(pl.BlockSpec(memory_space=pl.ANY))
    pairs = groups * count * BLOCK * (window + BLOCK)
    return pl.pallas_call(
        functools.partial(
            head_kernel, head, blocks, len(carry) // 2, closing, len(before), len(passing)
        ),
        grid_spec=pltpu.PrefetchScalarGridSpec(
            num_scalar_prefetch=1,
            grid=(1,),
            in_specs=in_specs,
            out_specs=out_specs,
            scratch_shapes=scratch,
        ),
        out_shape=out_shape,
        input_output_aliases=aliases,
        compiler_params=pltpu.CompilerParams(vmem_limit_bytes=VMEM_LIMIT),
        cost_estimate=pl.CostEstimate(
            flops=10 * pairs * head_dim, bytes_accessed=8 * tok_rows * head_dim * 2, transcendentals=pairs
        ),
        name="head_backward",
    )(me, queries, rims, keys, rims, values, lse, start, *cotans, *carry, *before, *passing)


def join_kernel(dk_tail_ref, dv_tail_ref, back_ref, dk_in, dv_in, dk_ref, dv_ref):
    dk_ref[0] = (dk_tail_ref[...] + back_ref[0].astype(F32)).astype(BF16)
    dv_ref[0] = (dv_tail_ref[...] + back_ref[1].astype(F32)).astype(BF16)


def join_call(head, dk_tail, dv_tail, back, grad_keys, grad_values):
    window, head_dim = dk_tail.shape
    last = grad_keys.shape[1] // window - 1
    tail = pl.BlockSpec((window, head_dim), lambda i: (0, 0))
    out = pl.BlockSpec((1, window, head_dim), lambda i: (head, last, 0))
    return pl.pallas_call(
        join_kernel,
        grid=(1,),
        in_specs=[
            tail,
            tail,
            pl.BlockSpec((2, window, head_dim), lambda i: (0, 0, 0)),
            pl.BlockSpec(memory_space=pl.ANY),
            pl.BlockSpec(memory_space=pl.ANY),
        ],
        out_specs=[out, out],
        out_shape=[jax.ShapeDtypeStruct(grad_keys.shape, BF16)] * 2,
        input_output_aliases={3: 0, 4: 1},
        name="join_tail",
    )(dk_tail, dv_tail, back, grad_keys, grad_values)


def body(queries, key_states, value_states, attn_output, out_cotangent, logsumexp, doc_start):
    kv_heads, tok_rows, head_dim = key_states.shape
    groups = queries.shape[0] // kv_heads
    pieces = lax.axis_size("head")
    me = lax.axis_index("head").astype(jnp.int32)[None]
    start = doc_start[None, :] - lax.axis_index("ctx") * tok_rows + W
    steps = tok_rows // BLOCK

    def sent(block, distance):
        route = [(i, (i + distance) % pieces) for i in range(pieces)]
        return lax.ppermute(block, "head", route)

    def packed(head, after):
        return pack_call(
            head, me, out_cotangent, attn_output, kv_heads, groups * head_dim, pieces, after
        )

    def arrived(parts):
        return [part if k == 0 else sent(part, k) for k, part in enumerate(parts)]

    parts = {0: packed(0, out_cotangent)}
    cotans = {0: arrived(parts[0])}
    rims = from_behind(rim_call(key_states, value_states, parts[0][0]), "ctx", 1)
    after = parts[0][0]
    for head in range(kv_heads - 1, 0, -1):
        parts[head] = packed(head, after)
        after = parts[head][0]
    if kv_heads > 1:
        cotans[1] = arrived(parts[1])

    before = []
    waiting = None
    for head in range(kv_heads):
        later = parts[head + 2] if head + 2 < kv_heads else []
        got = head_call(
            head, (0, steps), me, queries, rims, key_states, value_states,
            logsumexp, start, cotans[head], before, [], True, later[1:],
        )
        if later:
            cotans[head + 2] = arrived([later[0], *got[6:]])
        before = list(got[:3])
        if waiting is not None:
            before[1:] = join_call(*waiting, *before[1:])
        waiting = (head, got[3], got[4], from_behind(got[5], "ctx", -1))
    before[1:] = join_call(*waiting, *before[1:])
    return tuple(before)


def solution(mesh):
    return jax.shard_map(
        body,
        mesh=mesh,
        in_specs=(
            P("head", "ctx", None),
            P("head", "ctx", None),
            P("head", "ctx", None),
            P(("ctx", "head"), None),
            P(("ctx", "head"), None),
            P("head", "ctx"),
            P("ctx"),
        ),
        out_specs=(P("head", "ctx", None), P("head", "ctx", None), P("head", "ctx", None)),
        check_vma=False,
    )
```

time: 247 us -> 159 us (0.64)
  Pallas kernels: 156 us -> 95.3 us
  local copies, waits for them, and re-layouts: 20.7 us -> 6.01 us
  waiting for transfers between devices: 15 us -> 6.02 us
    pallas_call x5 -> x9, Pallas kernels: 148 us -> 86.5 us  [the longest x4 70.7 us: head_call(): pl.pallas_call(functools.partial(head_kernel, head, blocks, len(carry) //...]
    ppermute x15 -> x12, waiting for transfers between devices: 13.7 us -> 0.03 us  [sent(): return lax.ppermute(block, 'head', route)]
    ppermute x6 -> x5, starting transfers between devices: 19.5 us -> 13.5 us  [from_behind(): return lax.ppermute(block, axis, route)]
    unnamed x36 -> x40, local copies, waits for them, and re-layouts: 11.9 us -> 6.01 us
    dynamic_slice x2 -> x0, local copies, waits for them, and re-layouts: 5.28 us -> none  [the longest x1 3.91 us: body(): lax.dynamic_slice_in_dim(out_cotangent, target * width + head * cols, col...]
    ppermute x6 -> x5, waiting for transfers between devices: 1.38 us -> 5.98 us  [from_behind(): return lax.ppermute(block, axis, route)]
    ppermute x15 -> x12, starting transfers between devices: 31.2 us -> 35.6 us  [sent(): return lax.ppermute(block, 'head', route)]
    slice x2 -> x0, local copies, waits for them, and re-layouts: 3.46 us -> none  [the longest x1 2.42 us: body(): value_states[:, tok_rows - window:]]
  transfers between devices with their start and end apart: 21 -> 17, of which waited for: 4 -> 1; matrix products, arithmetic and copies ran while one was open for 3% -> 0% of each run, Pallas kernels for 63% -> 55%
where the time goes in v2:
time: 159 us; the launch traced here: 158 us
  Pallas kernels  95.3 us (60%)
  starting transfers between devices  49.1 us (31%)
  waiting for transfers between devices  6.02 us (4%)
  local copies, waits for them, and re-layouts  6.01 us (4%)
    pallas_call x4, Pallas kernels, head_call(): pl.pallas_call(functools.partial(head_kernel, head, blocks, len(carry) //...  70.7 us
    ppermute x12, starting transfers between devices, sent(): return lax.ppermute(block, 'head', route)  35.6 us
    ppermute x5, starting transfers between devices, from_behind(): return lax.ppermute(block, axis, route)  13.5 us
    pallas_call x4, Pallas kernels, pack_call(): pl.pallas_call(functools.partial(pack_kernel, pieces), grid_spec=pltpu.Pr...  12 us
    pallas_call x4, Pallas kernels, join_call(): pl.pallas_call(join_kernel, grid=(1,), in_specs=[tail, tail, pl.BlockSpec...  8.84 us
    unnamed x40, local copies, waits for them, and re-layouts  6.01 us
    ppermute x5, waiting for transfers between devices, from_behind(): return lax.ppermute(block, axis, route)  5.98 us
    pallas_call x1, Pallas kernels, rim_call(): pl.pallas_call(rim_kernel, grid=(kv_heads,), in_specs=[last, last, pl.Blo...  3.8 us
  transfers between devices with their start and end apart: 17, of which 1 were waited for; matrix products, arithmetic and copies ran while one was open for 0% of the time, Pallas kernels for 55%

profile of v2, /device:TPU:1, one launch (start us, length us, event | category | flops | bytes accessed | tf_op | source)
XLA Modules:
  0.0 157.9 jit_solution(5964194389086881008)
XLA Ops:
  0.6 3.0 %pack_cotangent.4 = (bf16[528,256]{1,0:T(8,128)(2,1)}, bf16[528,256]{1,0:T(8,128)(2,1)}, bf16[528,256]{1,0:T(8,128)(2,1)}, bf16[528,256]{1,0:T(8,128)(2,1)}) custom-call(s32[1]{0:T(128)} %bitcast.me_ref, bf16[512,4096]{1,0:T(8,128)(2,1)} %refs_3_.7, bf16[512,4096]{1,0:T(8,128)(2,1)} %refs_3_.7, bf16[512,4096]{1,0:T(8,128)(2,1)} %refs_3_.7, ...), custom_call_target="tpu_custom_call" | custom-call | flops 2097152 | bytes 3145728 | tf_op jit(solution)/shard_map/pack_cotangent/pallas_call | solution.py:72
  3.6 3.8 %rims.1 = bf16[2,4,1024,128]{3,2,1,0:T(8,128)(2,1)} custom-call(bf16[4,2048,128]{2,1,0:T(8,128)(2,1)} %refs_2_.15, bf16[4,2048,128]{2,1,0:T(8,128)(2,1)} %refs_4_.15, bf16[528,256]{1,0:T(8,128)(2,1)} %get-tuple-element.57.after_ref.refs_8_.refs_7_), custom_call_target="tpu_custom_call" | custom-call | tf_op jit(solution)/shard_map/rims/pallas_call | solution.py:98
  7.4 4.5 %collective-permute-start = (bf16[2,4,1024,128]{3,2,1,0:T(8,128)(2,1)}, bf16[2,4,1024,128]{3,2,1,0:T(8,128)(2,1)S(1)}, u32[]{:S(2)}, u32[]{:S(2)}) collective-permute-start(bf16[2,4,1024,128]{3,2,1,0:T(8,128)(2,1)} %rims.1), channel_id=1, source_target_pairs={{0,4},{4,8},{8,12},{12,16},{16,20},{20,24},{24,28},{1,5},{5,9},{9,... | collective-permute-start | bytes 6291464 | tf_op jit(solution)/shard_map/ppermute | solution.py:27
  13.3 2.3 %collective-permute-start.5 = (bf16[528,256]{1,0:T(8,128)(2,1)}, bf16[528,256]{1,0:T(8,128)(2,1)S(1)}, u32[]{:S(2)}, u32[]{:S(2)}) collective-permute-start(bf16[528,256]{1,0:T(8,128)(2,1)} %get-tuple-element.65), channel_id=1, source_target_pairs={{0,2},{1,3},{2,0},{3,1},{4,6},{5,7},{6,4},{7,5},{8,10},{9,11},{10,... | collective-permute-start | bytes 811016 | tf_op jit(solution)/shard_map/ppermute | solution.py:372
  16.7 3.0 %pack_cotangent.5 = (bf16[528,256]{1,0:T(8,128)(2,1)}, bf16[528,256]{1,0:T(8,128)(2,1)}, bf16[528,256]{1,0:T(8,128)(2,1)}, bf16[528,256]{1,0:T(8,128)(2,1)}) custom-call(s32[1]{0:T(128)} %bitcast.me_ref, bf16[512,4096]{1,0:T(8,128)(2,1)} %refs_3_.7, bf16[512,4096]{1,0:T(8,128)(2,1)} %refs_3_.7, bf16[512,4096]{1,0:T(8,128)(2,1)} %refs_3_.7, ...), custom_call_target="tpu_custom_call" | custom-call | flops 2097152 | bytes 3145728 | tf_op jit(solution)/shard_map/pack_cotangent/pallas_call | solution.py:72
  19.6 3.0 %pack_cotangent.6 = (bf16[528,256]{1,0:T(8,128)(2,1)}, bf16[528,256]{1,0:T(8,128)(2,1)}, bf16[528,256]{1,0:T(8,128)(2,1)}, bf16[528,256]{1,0:T(8,128)(2,1)}) custom-call(s32[1]{0:T(128)} %bitcast.me_ref, bf16[512,4096]{1,0:T(8,128)(2,1)} %refs_3_.7, bf16[512,4096]{1,0:T(8,128)(2,1)} %refs_3_.7, bf16[512,4096]{1,0:T(8,128)(2,1)} %refs_3_.7, ...), custom_call_target="tpu_custom_call" | custom-call | flops 2097152 | bytes 3145728 | tf_op jit(solution)/shard_map/pack_cotangent/pallas_call | solution.py:72
  22.7 3.0 %pack_cotangent.7 = (bf16[528,256]{1,0:T(8,128)(2,1)}, bf16[528,256]{1,0:T(8,128)(2,1)}, bf16[528,256]{1,0:T(8,128)(2,1)}, bf16[528,256]{1,0:T(8,128)(2,1)}) custom-call(s32[1]{0:T(128)} %bitcast.me_ref, bf16[512,4096]{1,0:T(8,128)(2,1)} %refs_3_.7, bf16[512,4096]{1,0:T(8,128)(2,1)} %refs_3_.7, bf16[512,4096]{1,0:T(8,128)(2,1)} %refs_3_.7, ...), custom_call_target="tpu_custom_call" | custom-call | flops 2097152 | bytes 3145728 | tf_op jit(solution)/shard_map/pack_cotangent/pallas_call | solution.py:72
  26.6 7.6 %collective-permute-start.2 = (bf16[528,256]{1,0:T(8,128)(2,1)}, bf16[528,256]{1,0:T(8,128)(2,1)S(1)}, u32[]{:S(2)}, u32[]{:S(2)}) collective-permute-start(bf16[528,256]{1,0:T(8,128)(2,1)} %get-tuple-element.62), channel_id=1, source_target_pairs={{0,2},{1,3},{2,0},{3,1},{4,6},{5,7},{6,4},{7,5},{8,10},{9,11},{10,... | collective-permute-start | bytes 811016 | tf_op jit(solution)/shard_map/ppermute | solution.py:372
  34.3 15.4 %collective-permute-start.3 = (bf16[528,256]{1,0:T(8,128)(2,1)}, bf16[528,256]{1,0:T(8,128)(2,1)S(1)}, u32[]{:S(2)}, u32[]{:S(2)}) collective-permute-start(bf16[528,256]{1,0:T(8,128)(2,1)} %get-tuple-element.63), channel_id=1, source_target_pairs={{0,3},{1,0},{2,1},{3,2},{4,7},{5,4},{6,5},{7,6},{8,11},{9,8},{10,9... | collective-permute-start | bytes 811016 | tf_op jit(solution)/shard_map/ppermute | solution.py:372
  51.1 17.7 %head_backward.4 = (bf16[8,2048,128]{2,1,0:T(8,128)(2,1)}, bf16[4,2048,128]{2,1,0:T(8,128)(2,1)}, bf16[4,2048,128]{2,1,0:T(8,128)(2,1)}, f32[1024,128]{1,0:T(8,1...) custom-call(s32[1]{0:T(128)} %bitcast.me_ref, ...), custom_call_target="tpu_custom_call", output_to_operand_aliasing={{6}: (12, {}), {7}: (13, {}), {8}: (14, {})} | custom-call | flops 6039797760 | bytes 4194304 | tf_op jit(solution)/shard_map/head_backward/pallas_call | solution.py:314
  69.9 2.1 %collective-permute-start.12 = (bf16[528,256]{1,0:T(8,128)(2,1)}, bf16[528,256]{1,0:T(8,128)(2,1)S(1)}, u32[]{:S(2)}, u32[]{:S(2)}) collective-permute-start(bf16[528,256]{1,0:T(8,128)(2,1)} %get-tuple-element.81), channel_id=1, source_target_pairs={{0,3},{1,0},{2,1},{3,2},{4,7},{5,4},{6,5},{7,6},{8,11},{9,8},{10,9... | collective-permute-start | bytes 811016 | tf_op jit(solution)/shard_map/ppermute | solution.py:372
  72.1 3.0 %collective-permute-start.13 = (bf16[2,1024,128]{2,1,0:T(8,128)(2,1)}, bf16[2,1024,128]{2,1,0:T(8,128)(2,1)S(1)}, u32[]{:S(2)}, u32[]{:S(2)}) collective-permute-start(bf16[2,1024,128]{2,1,0:T(8,128)(2,1)} %get-tuple-element.85), channel_id=1, source_target_pairs={{4,0},{8,4},{12,8},{16,12},{20,16},{24,20},{28,24},{5,1},{9,5},{13... | collective-permute-start | bytes 1572872 | tf_op jit(solution)/shard_map/ppermute | solution.py:27
  75.9 17.7 %head_backward.5 = (bf16[8,2048,128]{2,1,0:T(8,128)(2,1)}, bf16[4,2048,128]{2,1,0:T(8,128)(2,1)}, bf16[4,2048,128]{2,1,0:T(8,128)(2,1)}, f32[1024,128]{1,0:T(8,1...) custom-call(s32[1]{0:T(128)} %bitcast.me_ref, ...), custom_call_target="tpu_custom_call", output_to_operand_aliasing={{0}: (12, {}), {1}: (13, {}), {2}: (14, {}), {6}: (15, {}),... | custom-call | flops 6039797760 | bytes 4194304 | tf_op jit(solution)/shard_map/head_backward/pallas_call | solution.py:314
  93.6 2.0 %collective-permute-start.8 = (bf16[528,256]{1,0:T(8,128)(2,1)}, bf16[528,256]{1,0:T(8,128)(2,1)S(1)}, u32[]{:S(2)}, u32[]{:S(2)}) collective-permute-start(bf16[528,256]{1,0:T(8,128)(2,1)} %get-tuple-element.77), channel_id=1, source_target_pairs={{0,2},{1,3},{2,0},{3,1},{4,6},{5,7},{6,4},{7,5},{8,10},{9,11},{10,... | collective-permute-start | bytes 811016 | tf_op jit(solution)/shard_map/ppermute | solution.py:372
  95.5 2.3 %join_tail.4 = (bf16[4,2048,128]{2,1,0:T(8,128)(2,1)}, bf16[4,2048,128]{2,1,0:T(8,128)(2,1)}) custom-call(f32[1024,128]{1,0:T(8,128)} %get-tuple-element.83.dk_tail_ref, f32[1024,128]{1,0:T(8,128)} %get-tuple-element.84.dv_tail_ref, bf16[2,1024,128]{2,1,0:T(8,128)(2,1)} %copy-done.2, ...), custom_call_target="tpu_custom_call", output_to_operand_aliasing={{0}: (3, {}), {1}: (4, {})} | custom-call | tf_op jit(solution)/shard_map/join_tail/pallas_call | solution.py:345
  97.8 2.1 %collective-permute-start.9 = (bf16[528,256]{1,0:T(8,128)(2,1)S(1)}, bf16[528,256]{1,0:T(8,128)(2,1)}, u32[]{:S(2)}, u32[]{:S(2)}) collective-permute-start(bf16[528,256]{1,0:T(8,128)(2,1)S(1)} %copy-done.5), channel_id=1, source_target_pairs={{0,3},{1,0},{2,1},{3,2},{4,7},{5,4},{6,5},{7,6},{8,11},{9,8},{10,9... | collective-permute-start | bytes 811016 | tf_op jit(solution)/shard_map/ppermute | solution.py:372
  100.0 1.9 %collective-permute-start.14 = (bf16[2,1024,128]{2,1,0:T(8,128)(2,1)S(1)}, bf16[2,1024,128]{2,1,0:T(8,128)(2,1)S(1)}, u32[]{:S(2)}, u32[]{:S(2)}) collective-permute-start(bf16[2,1024,128]{2,1,0:T(8,128)(2,1)S(1)} %copy-done.10), channel_id=1, source_target_pairs={{4,0},{8,4},{12,8},{16,12},{20,16},{24,20},{28,24},{5,1},{9,5},{13... | collective-permute-start | bytes 1572872 | tf_op jit(solution)/shard_map/ppermute | solution.py:27
  102.6 17.7 %head_backward.6 = (bf16[8,2048,128]{2,1,0:T(8,128)(2,1)}, bf16[4,2048,128]{2,1,0:T(8,128)(2,1)}, bf16[4,2048,128]{2,1,0:T(8,128)(2,1)}, f32[1024,128]{1,0:T(8,1...) custom-call(s32[1]{0:T(128)} %bitcast.me_ref, ...), custom_call_target="tpu_custom_call", output_to_operand_aliasing={{0}: (12, {}), {1}: (13, {}), {2}: (14, {})} | custom-call | flops 6039797760 | bytes 4194304 | tf_op jit(solution)/shard_map/head_backward/pallas_call | solution.py:314
  120.3 2.1 %collective-permute-start.16 = (bf16[2,1024,128]{2,1,0:T(8,128)(2,1)}, bf16[2,1024,128]{2,1,0:T(8,128)(2,1)S(1)}, u32[]{:S(2)}, u32[]{:S(2)}) collective-permute-start(bf16[2,1024,128]{2,1,0:T(8,128)(2,1)} %get-tuple-element.104), channel_id=1, source_target_pairs={{4,0},{8,4},{12,8},{16,12},{20,16},{24,20},{28,24},{5,1},{9,5},{13... | collective-permute-start | bytes 1572872 | tf_op jit(solution)/shard_map/ppermute | solution.py:27
  123.3 2.2 %join_tail.5 = (bf16[4,2048,128]{2,1,0:T(8,128)(2,1)}, bf16[4,2048,128]{2,1,0:T(8,128)(2,1)}) custom-call(f32[1024,128]{1,0:T(8,128)} %get-tuple-element.91.dk_tail_ref, f32[1024,128]{1,0:T(8,128)} %get-tuple-element.92.dv_tail_ref, bf16[2,1024,128]{2,1,0:T(8,128)(2,1)} %copy-done.3, ...), custom_call_target="tpu_custom_call", output_to_operand_aliasing={{0}: (3, {}), {1}: (4, {})} | custom-call | tf_op jit(solution)/shard_map/join_tail/pallas_call | solution.py:345
  126.3 17.7 %head_backward.7 = (bf16[8,2048,128]{2,1,0:T(8,128)(2,1)}, bf16[4,2048,128]{2,1,0:T(8,128)(2,1)}, bf16[4,2048,128]{2,1,0:T(8,128)(2,1)}, f32[1024,128]{1,0:T(8,1...) custom-call(s32[1]{0:T(128)} %bitcast.me_ref, ...), custom_call_target="tpu_custom_call", output_to_operand_aliasing={{0}: (12, {}), {1}: (13, {}), {2}: (14, {})} | custom-call | flops 6039797760 | bytes 4194304 | tf_op jit(solution)/shard_map/head_backward/pallas_call | solution.py:314
  146.7 2.2 %join_tail.6 = (bf16[4,2048,128]{2,1,0:T(8,128)(2,1)}, bf16[4,2048,128]{2,1,0:T(8,128)(2,1)}) custom-call(f32[1024,128]{1,0:T(8,128)} %get-tuple-element.102.dk_tail_ref, f32[1024,128]{1,0:T(8,128)} %get-tuple-element.103.dv_tail_ref, bf16[2,1024,128]{2,1,0:T(8,128)(2,1)} %copy-done.1, ...), custom_call_target="tpu_custom_call", output_to_operand_aliasing={{0}: (3, {}), {1}: (4, {})} | custom-call | tf_op jit(solution)/shard_map/join_tail/pallas_call | solution.py:345
  148.9 6.0 %collective-permute-done.15.back_ref = bf16[2,1024,128]{2,1,0:T(8,128)(2,1)S(1)} collective-permute-done((bf16[2,1024,128]{2,1,0:T(8,128)(2,1)}, bf16[2,1024,128]{2,1,0:T(8,128)(2,1)S(1)}, u32[]{:S(2)}, u32[]{:S(2)}) %collective-permute-start.15) | collective-permute-done | bytes 524320 | tf_op jit(solution)/shard_map/ppermute | solution.py:27
  155.7 2.2 %join_tail.7 = (bf16[4,2048,128]{2,1,0:T(8,128)(2,1)}, bf16[4,2048,128]{2,1,0:T(8,128)(2,1)}) custom-call(f32[1024,128]{1,0:T(8,128)} %get-tuple-element.99.dk_tail_ref, f32[1024,128]{1,0:T(8,128)} %get-tuple-element.100.dv_tail_ref, bf16[2,1024,128]{2,1,0:T(8,128)(2,1)} %copy-done.4, ...), custom_call_target="tpu_custom_call", output_to_operand_aliasing={{0}: (3, {}), {1}: (4, {})} | custom-call | tf_op jit(solution)/shard_map/join_tail/pallas_call | solution.py:345
  (64 shorter events, 12.6 us)
Async XLA Ops:
  3.6 12.0 %copy-start.19 = (bf16[528,256]{1,0:T(8,128)(2,1)S(1)}, bf16[528,256]{1,0:T(8,128)(2,1)}, u32[]{:S(2)}) copy-start(bf16[528,256]{1,0:T(8,128)(2,1)} %get-tuple-element.66) | copy-start | bytes 811012
  7.4 42.3 %collective-permute-start = (bf16[2,4,1024,128]{3,2,1,0:T(8,128)(2,1)}, bf16[2,4,1024,128]{3,2,1,0:T(8,128)(2,1)S(1)}, u32[]{:S(2)}, u32[]{:S(2)}) collective-permute-start(bf16[2,4,1024,128]{3,2,1,0:T(8,128)(2,1)} %rims.1), channel_id=1, source_target_pairs={{0,4},{4,8},{8,12},{12,16},{16,20},{20,24},{24,28},{1,5},{5,9},{9,... | collective-permute-start | bytes 6291464 | tf_op jit(solution)/shard_map/ppermute | solution.py:27
  11.9 14.7 %collective-permute-start.4 = (bf16[528,256]{1,0:T(8,128)(2,1)}, bf16[528,256]{1,0:T(8,128)(2,1)S(1)}, u32[]{:S(2)}, u32[]{:S(2)}) collective-permute-start(bf16[528,256]{1,0:T(8,128)(2,1)} %get-tuple-element.64), channel_id=1, source_target_pairs={{0,1},{1,2},{2,3},{3,0},{4,5},{5,6},{6,7},{7,4},{8,9},{9,10},{10,1... | collective-permute-start | bytes 811016 | tf_op jit(solution)/shard_map/ppermute | solution.py:372
  13.3 21.0 %collective-permute-start.5 = (bf16[528,256]{1,0:T(8,128)(2,1)}, bf16[528,256]{1,0:T(8,128)(2,1)S(1)}, u32[]{:S(2)}, u32[]{:S(2)}) collective-permute-start(bf16[528,256]{1,0:T(8,128)(2,1)} %get-tuple-element.65), channel_id=1, source_target_pairs={{0,2},{1,3},{2,0},{3,1},{4,6},{5,7},{6,4},{7,5},{8,10},{9,11},{10,... | collective-permute-start | bytes 811016 | tf_op jit(solution)/shard_map/ppermute | solution.py:372
  15.6 34.1 %collective-permute-start.6 = (bf16[528,256]{1,0:T(8,128)(2,1)S(1)}, bf16[528,256]{1,0:T(8,128)(2,1)S(1)}, u32[]{:S(2)}, u32[]{:S(2)}) collective-permute-start(bf16[528,256]{1,0:T(8,128)(2,1)S(1)} %copy-done.19), channel_id=1, source_target_pairs={{0,3},{1,0},{2,1},{3,2},{4,7},{5,4},{6,5},{7,6},{8,11},{9,8},{10,9... | collective-permute-start | bytes 811016 | tf_op jit(solution)/shard_map/ppermute | solution.py:372
  22.7 3.4 %copy-start.9 = (s32[2048]{0:T(1024)S(1)}, s32[2048]{0:T(1024)}, u32[]{:S(2)}) copy-start(s32[2048]{0:T(1024)} %param.13) | copy-start | bytes 24580
  25.6 44.3 %collective-permute-start.1 = (bf16[528,256]{1,0:T(8,128)(2,1)}, bf16[528,256]{1,0:T(8,128)(2,1)S(1)}, u32[]{:S(2)}, u32[]{:S(2)}) collective-permute-start(bf16[528,256]{1,0:T(8,128)(2,1)} %get-tuple-element.61), channel_id=1, source_target_pairs={{0,1},{1,2},{2,3},{3,0},{4,5},{5,6},{6,7},{7,4},{8,9},{9,10},{10,1... | collective-permute-start | bytes 811016 | tf_op jit(solution)/shard_map/ppermute | solution.py:372
  26.6 23.0 %copy-start.16 = (bf16[528,256]{1,0:T(8,128)(2,1)}, bf16[528,256]{1,0:T(8,128)(2,1)S(1)}, u32[]{:S(2)}) copy-start(bf16[528,256]{1,0:T(8,128)(2,1)S(1)} %collective-permute-done.4.refs_8_) | copy-start | bytes 811012
  26.6 45.4 %collective-permute-start.2 = (bf16[528,256]{1,0:T(8,128)(2,1)}, bf16[528,256]{1,0:T(8,128)(2,1)S(1)}, u32[]{:S(2)}, u32[]{:S(2)}) collective-permute-start(bf16[528,256]{1,0:T(8,128)(2,1)} %get-tuple-element.62), channel_id=1, source_target_pairs={{0,2},{1,3},{2,0},{3,1},{4,6},{5,7},{6,4},{7,5},{8,10},{9,11},{10,... | collective-permute-start | bytes 811016 | tf_op jit(solution)/shard_map/ppermute | solution.py:372
  34.3 15.4 %copy-start.17 = (bf16[528,256]{1,0:T(8,128)(2,1)}, bf16[528,256]{1,0:T(8,128)(2,1)S(1)}, u32[]{:S(2)}) copy-start(bf16[528,256]{1,0:T(8,128)(2,1)S(1)} %collective-permute-done.5.refs_9_) | copy-start | bytes 811012
  34.3 40.8 %collective-permute-start.3 = (bf16[528,256]{1,0:T(8,128)(2,1)}, bf16[528,256]{1,0:T(8,128)(2,1)S(1)}, u32[]{:S(2)}, u32[]{:S(2)}) collective-permute-start(bf16[528,256]{1,0:T(8,128)(2,1)} %get-tuple-element.63), channel_id=1, source_target_pairs={{0,3},{1,0},{2,1},{3,2},{4,7},{5,4},{6,5},{7,6},{8,11},{9,8},{10,9... | collective-permute-start | bytes 811016 | tf_op jit(solution)/shard_map/ppermute | solution.py:372
  68.7 29.1 %collective-permute-start.10 = (bf16[528,256]{1,0:T(8,128)(2,1)}, bf16[528,256]{1,0:T(8,128)(2,1)S(1)}, u32[]{:S(2)}, u32[]{:S(2)}) collective-permute-start(bf16[528,256]{1,0:T(8,128)(2,1)} %get-tuple-element.79), channel_id=1, source_target_pairs={{0,1},{1,2},{2,3},{3,0},{4,5},{5,6},{6,7},{7,4},{8,9},{9,10},{10,1... | collective-permute-start | bytes 811016 | tf_op jit(solution)/shard_map/ppermute | solution.py:372
  69.9 30.0 %collective-permute-start.11 = (bf16[528,256]{1,0:T(8,128)(2,1)}, bf16[528,256]{1,0:T(8,128)(2,1)S(1)}, u32[]{:S(2)}, u32[]{:S(2)}) collective-permute-start(bf16[528,256]{1,0:T(8,128)(2,1)} %get-tuple-element.80), channel_id=1, source_target_pairs={{0,2},{1,3},{2,0},{3,1},{4,6},{5,7},{6,4},{7,5},{8,10},{9,11},{10,... | collective-permute-start | bytes 811016 | tf_op jit(solution)/shard_map/ppermute | solution.py:372
  69.9 5.2 %copy-start.6 = (bf16[528,256]{1,0:T(8,128)(2,1)}, bf16[528,256]{1,0:T(8,128)(2,1)S(1)}, u32[]{:S(2)}) copy-start(bf16[528,256]{1,0:T(8,128)(2,1)S(1)} %collective-permute-done.1.refs_8_) | copy-start | bytes 811012
  69.9 31.9 %collective-permute-start.12 = (bf16[528,256]{1,0:T(8,128)(2,1)}, bf16[528,256]{1,0:T(8,128)(2,1)S(1)}, u32[]{:S(2)}, u32[]{:S(2)}) collective-permute-start(bf16[528,256]{1,0:T(8,128)(2,1)} %get-tuple-element.81), channel_id=1, source_target_pairs={{0,3},{1,0},{2,1},{3,2},{4,7},{5,4},{6,5},{7,6},{8,11},{9,8},{10,9... | collective-permute-start | bytes 811016 | tf_op jit(solution)/shard_map/ppermute | solution.py:372
  72.1 21.5 %collective-permute-start.13 = (bf16[2,1024,128]{2,1,0:T(8,128)(2,1)}, bf16[2,1024,128]{2,1,0:T(8,128)(2,1)S(1)}, u32[]{:S(2)}, u32[]{:S(2)}) collective-permute-start(bf16[2,1024,128]{2,1,0:T(8,128)(2,1)} %get-tuple-element.85), channel_id=1, source_target_pairs={{4,0},{8,4},{12,8},{16,12},{20,16},{24,20},{28,24},{5,1},{9,5},{13... | collective-permute-start | bytes 1572872 | tf_op jit(solution)/shard_map/ppermute | solution.py:27
  93.6 31.9 %collective-permute-start.7 = (bf16[528,256]{1,0:T(8,128)(2,1)}, bf16[528,256]{1,0:T(8,128)(2,1)S(1)}, u32[]{:S(2)}, u32[]{:S(2)}) collective-permute-start(bf16[528,256]{1,0:T(8,128)(2,1)} %get-tuple-element.76), channel_id=1, source_target_pairs={{0,1},{1,2},{2,3},{3,0},{4,5},{5,6},{6,7},{7,4},{8,9},{9,10},{10,1... | collective-permute-start | bytes 811016 | tf_op jit(solution)/shard_map/ppermute | solution.py:372
  93.6 31.9 %collective-permute-start.8 = (bf16[528,256]{1,0:T(8,128)(2,1)}, bf16[528,256]{1,0:T(8,128)(2,1)S(1)}, u32[]{:S(2)}, u32[]{:S(2)}) collective-permute-start(bf16[528,256]{1,0:T(8,128)(2,1)} %get-tuple-element.77), channel_id=1, source_target_pairs={{0,2},{1,3},{2,0},{3,1},{4,6},{5,7},{6,4},{7,5},{8,10},{9,11},{10,... | collective-permute-start | bytes 811016 | tf_op jit(solution)/shard_map/ppermute | solution.py:372
  95.5 4.4 %copy-start.10 = (bf16[2,1024,128]{2,1,0:T(8,128)(2,1)S(1)}, bf16[2,1024,128]{2,1,0:T(8,128)(2,1)}, u32[]{:S(2)}) copy-start(bf16[2,1024,128]{2,1,0:T(8,128)(2,1)} %get-tuple-element.93) | copy-start | bytes 1572868
  97.8 4.1 %copy-start.11 = (bf16[528,256]{1,0:T(8,128)(2,1)}, bf16[528,256]{1,0:T(8,128)(2,1)S(1)}, u32[]{:S(2)}) copy-start(bf16[528,256]{1,0:T(8,128)(2,1)S(1)} %collective-permute-done.10.refs_8_) | copy-start | bytes 811012
  97.8 27.7 %collective-permute-start.9 = (bf16[528,256]{1,0:T(8,128)(2,1)S(1)}, bf16[528,256]{1,0:T(8,128)(2,1)}, u32[]{:S(2)}, u32[]{:S(2)}) collective-permute-start(bf16[528,256]{1,0:T(8,128)(2,1)S(1)} %copy-done.5), channel_id=1, source_target_pairs={{0,3},{1,0},{2,1},{3,2},{4,7},{5,4},{6,5},{7,6},{8,11},{9,8},{10,9... | collective-permute-start | bytes 811016 | tf_op jit(solution)/shard_map/ppermute | solution.py:372
  100.0 22.5 %collective-permute-start.14 = (bf16[2,1024,128]{2,1,0:T(8,128)(2,1)S(1)}, bf16[2,1024,128]{2,1,0:T(8,128)(2,1)S(1)}, u32[]{:S(2)}, u32[]{:S(2)}) collective-permute-start(bf16[2,1024,128]{2,1,0:T(8,128)(2,1)S(1)} %copy-done.10), channel_id=1, source_target_pairs={{4,0},{8,4},{12,8},{16,12},{20,16},{24,20},{28,24},{5,1},{9,5},{13... | collective-permute-start | bytes 1572872 | tf_op jit(solution)/shard_map/ppermute | solution.py:27
  120.3 25.6 %collective-permute-start.16 = (bf16[2,1024,128]{2,1,0:T(8,128)(2,1)}, bf16[2,1024,128]{2,1,0:T(8,128)(2,1)S(1)}, u32[]{:S(2)}, u32[]{:S(2)}) collective-permute-start(bf16[2,1024,128]{2,1,0:T(8,128)(2,1)} %get-tuple-element.104), channel_id=1, source_target_pairs={{4,0},{8,4},{12,8},{16,12},{20,16},{24,20},{28,24},{5,1},{9,5},{13... | collective-permute-start | bytes 1572872 | tf_op jit(solution)/shard_map/ppermute | solution.py:27
  144.0 10.9 %collective-permute-start.15 = (bf16[2,1024,128]{2,1,0:T(8,128)(2,1)}, bf16[2,1024,128]{2,1,0:T(8,128)(2,1)S(1)}, u32[]{:S(2)}, u32[]{:S(2)}) collective-permute-start(bf16[2,1024,128]{2,1,0:T(8,128)(2,1)} %get-tuple-element.101), channel_id=1, source_target_pairs={{4,0},{8,4},{12,8},{16,12},{20,16},{24,20},{28,24},{5,1},{9,5},{13... | collective-permute-start | bytes 1572872 | tf_op jit(solution)/shard_map/ppermute | solution.py:27
  (13 other events, 16.8 us)

commit v3 on v2

v3 whole, which is shorter than its diff:
```python
import functools
import math

import jax
import jax.numpy as jnp
from jax import lax
from jax.experimental import pallas as pl
from jax.experimental.pallas import tpu as pltpu
from jax.sharding import PartitionSpec as P

W = 1024
QPRE = 168
BLOCK = 128
SUB = 32
UNROLL = 4
VMEM_LIMIT = 56 * 1024 * 1024
LOG2E = math.log2(math.e)
F32 = jnp.float32
BF16 = jnp.bfloat16
NT = (((1,), (1,)), ((), ()))
NN = (((1,), (0,)), ((), ()))


def from_behind(block, axis, distance):
    devices = range(lax.axis_size(axis))
    route = [(i - distance, i) for i in devices if i - distance in devices]
    return lax.ppermute(block, axis, route)


def pack_kernel(pieces, ends, me_ref, *refs):
    cotan_refs, output_refs = refs[:pieces], refs[pieces : 2 * pieces]
    end_refs = refs[2 * pieces : 2 * pieces + ends]
    refs = refs[2 * pieces + ends + 1 :]
    out_refs, rows_ref = refs[:pieces], refs[-1]
    for i in range(ends):
        refs[pieces][i] = end_refs[i][...]
    rows, cols = cotan_refs[0].shape
    groups = cols // BLOCK
    in_piece = rows // BLOCK
    head_of = lax.broadcasted_iota(jnp.int32, (16, cols), 1) // BLOCK
    member = (head_of == lax.broadcasted_iota(jnp.int32, (16, cols), 0)).astype(BF16)
    rows_ref[...] = jnp.zeros_like(rows_ref)
    for k in range(pieces):
        cotan = cotan_refs[k][...]
        product = cotan.astype(F32) * output_refs[k][...].astype(F32)
        high = product.astype(BF16)
        low = (product - high.astype(F32)).astype(BF16)
        delta = lax.dot_general(member, high, NT, preferred_element_type=F32)
        delta = delta + lax.dot_general(member, low, NT, preferred_element_type=F32)
        out_refs[k][:rows] = cotan
        for part in range(3):
            rounded = delta.astype(BF16).astype(F32)
            delta = delta - rounded
            for j in range(in_piece):
                for i in range(groups):
                    rows_ref[
                        part * in_piece + j : part * in_piece + j + 1, i * BLOCK : (i + 1) * BLOCK
                    ] = rounded[i : i + 1, j * BLOCK : (j + 1) * BLOCK]
        out_refs[k][rows:] = rows_ref[...].astype(BF16)


def pack_call(head, me, cotan, output, kv_heads, cols, pieces, after, ends=(), ends_of=0):
    rows = cotan.shape[0]
    assert 3 * (rows // BLOCK) <= 16

    def piece_at(k):
        return pl.BlockSpec(
            (rows, cols), lambda i, me: (0, lax.rem(me[0] + k, pieces) * kv_heads + head)
        )

    in_specs = [piece_at(k) for k in range(pieces)] * 2
    for array in ends:
        last = array.shape[1] // W - 1
        in_specs += [pl.BlockSpec((ends_of, W, array.shape[2]), lambda i, me: (0, last, 0))]
    in_specs += [pl.BlockSpec(memory_space=pl.ANY)]
    operands = [cotan] * pieces + [output] * pieces + [*ends, after]
    out_specs = [pl.BlockSpec((rows + 16, cols), lambda i, me: (0, 0))] * pieces
    out_shape = [jax.ShapeDtypeStruct((rows + 16, cols), BF16)] * pieces
    if ends:
        shape = (len(ends), ends_of, W, ends[0].shape[2])
        out_specs += [pl.BlockSpec(shape, lambda i, me: (0, 0, 0, 0))]
        out_shape += [jax.ShapeDtypeStruct(shape, BF16)]
    scratch = [pltpu.VMEM((16, cols), F32)]
    return pl.pallas_call(
        functools.partial(pack_kernel, pieces, len(ends)),
        grid_spec=pltpu.PrefetchScalarGridSpec(
            num_scalar_prefetch=1,
            grid=(1,),
            in_specs=in_specs,
            out_specs=out_specs,
            scratch_shapes=scratch,
        ),
        out_shape=out_shape,
        compiler_params=pltpu.CompilerParams(vmem_limit_bytes=VMEM_LIMIT),
        cost_estimate=pl.CostEstimate(
            flops=4 * rows * cols * pieces, bytes_accessed=6 * rows * cols * pieces, transcendentals=0
        ),
        name="pack_cotangent",
    )(me, *operands)


def rim_kernel(key_ref, value_ref, after_ref, out_ref):
    out_ref[0] = key_ref[...]
    out_ref[1] = value_ref[...]


def rim_call(keys, values, from_head, after):
    kv_heads, tok_rows, head_dim = keys.shape
    last = pl.BlockSpec((1, W, head_dim), lambda i: (i + from_head, tok_rows // W - 1, 0))
    return pl.pallas_call(
        rim_kernel,
        grid=(kv_heads - from_head,),
        in_specs=[last, last, pl.BlockSpec(memory_space=pl.ANY)],
        out_specs=pl.BlockSpec((2, 1, W, head_dim), lambda i: (0, i, 0, 0)),
        out_shape=jax.ShapeDtypeStruct((2, kv_heads - from_head, W, head_dim), BF16),
        name="rims",
    )(keys, values, after)


def head_kernel(head, blocks, carried, aliased, passed, me_ref, *refs):
    q_ref, kh_ref, ko_ref, vh_ref, vo_ref, lse_ref, start_ref = refs[:7]
    groups, _, head_dim = q_ref.shape
    window = kh_ref.shape[0]
    tok_rows = ko_ref.shape[1]
    first_block, count = blocks
    opening = first_block == 0
    closing = first_block + count == tok_rows // BLOCK
    outputs = 1 + (4 if closing else 2) + opening
    pieces = len(refs) - 7 - 2 * carried - aliased - 2 * passed - outputs - 8
    cotan_refs = refs[7 : 7 + pieces]
    refs = refs[7 + pieces :]
    carry_refs = refs[: 2 * carried]
    refs = refs[2 * carried + aliased + passed :]
    dq_ref = refs[0]
    k_all, v_all, kt_all, cotan_all, delta_all, ds_all, dk_all, dv_all = refs[outputs + passed :]
    piece_rows = tok_rows // pieces
    in_piece = piece_rows // BLOCK
    span = window + BLOCK
    cols = groups * BLOCK
    scale = QPRE ** (-0.5)
    me = me_ref[0]
    base = first_block * BLOCK
    extent = k_all.shape[0]
    in_rim = max(window - base, 0)

    for all_ref, rim_ref, own_ref in ((k_all, kh_ref, ko_ref), (v_all, vh_ref, vo_ref)):
        if in_rim:
            all_ref[:in_rim] = rim_ref[base:]
        skip = base + in_rim - window
        all_ref[in_rim:] = own_ref[0, skip : skip + extent - in_rim]
    unit = (
        lax.broadcasted_iota(jnp.int32, (head_dim, head_dim), 0)
        == lax.broadcasted_iota(jnp.int32, (head_dim, head_dim), 1)
    ).astype(BF16)
    kt_all[...] = lax.dot_general(unit, k_all[...], NT, preferred_element_type=F32).astype(BF16)
    dk_all[...] = jnp.zeros_like(dk_all)
    dv_all[...] = jnp.zeros_like(dv_all)
    for all_ref, carry_ref in zip((dk_all, dv_all), carry_refs):
        all_ref[: carry_ref.shape[0]] = carry_ref[...]
    ds_all[...] = jnp.zeros_like(ds_all)
    for i in range(pieces):
        source = lax.rem(me - i + pieces, pieces)
        where = pl.ds(pl.multiple_of(source * piece_rows, piece_rows), piece_rows)
        for j in range(groups):
            cotan_all[j, where, :] = cotan_refs[i][:piece_rows, j * head_dim : (j + 1) * head_dim]
        parts = cotan_refs[i][piece_rows:].astype(F32)
        for j in range(in_piece):
            row = parts[j : j + 1] + parts[in_piece + j : in_piece + j + 1]
            delta_all[source * in_piece + j] = row + parts[2 * in_piece + j : 2 * in_piece + j + 1]

    def write_query(first, slot):
        dq = lax.dot_general(
            kt_all[:, pl.ds(first, span)], ds_all[slot], NN, preferred_element_type=F32
        )
        dq = (dq.T * F32(scale)).astype(BF16)
        dq_ref[:, pl.ds(first, BLOCK), :] = dq.reshape(groups, BLOCK, head_dim)

    token = lax.broadcasted_iota(jnp.int32, (1, cols), 1) % BLOCK
    place = lax.broadcasted_iota(jnp.int32, (SUB, cols), 0)
    chunks = span // BLOCK
    unroll = ds_all.shape[0]

    def load(index):
        first = pl.multiple_of(index * BLOCK, BLOCK)
        token_first = pl.multiple_of(base + first, BLOCK)
        here = pl.ds(token_first, BLOCK)
        query = q_ref[:, pl.ds(first, BLOCK), :].reshape(cols, head_dim)
        cotan = cotan_all[:, here, :].reshape(cols, head_dim)
        rows = [lse_ref[head * groups + i : head * groups + i + 1, here] for i in range(groups)]
        lse = jnp.concatenate(rows, axis=1) * F32(LOG2E)
        delta = delta_all[first_block + index]
        start = jnp.concatenate([start_ref[:, here]] * groups, axis=1) - token_first
        lower = jnp.maximum(start, token + 1)
        return first, query, cotan, lse, delta, lower

    def span_of(first, i):
        return pl.ds(pl.multiple_of(first + i * BLOCK, BLOCK), BLOCK)

    def front(block, i):
        first, query, cotan = block[:3]
        rows = span_of(first, i)
        return (
            lax.dot_general(k_all[rows, :], query, NT, preferred_element_type=F32),
            lax.dot_general(v_all[rows, :], cotan, NT, preferred_element_type=F32),
        )

    def back(block, i, probs_low, dscores):
        first, query, cotan = block[:3]
        rows = span_of(first, i)
        dv_all[rows, :] += lax.dot_general(probs_low, cotan, NN, preferred_element_type=F32)
        dk_all[rows, :] += lax.dot_general(dscores, query, NN, preferred_element_type=F32)

    def middle(block, slot, i, scores, dprobs):
        _, _, _, lse, delta, lower = block
        lows = []
        for at in range(0, BLOCK, SUB):
            part = slice(at, at + SUB)
            shift = i * BLOCK + at
            allowed = place >= lower - shift
            if shift + SUB > window:
                allowed = allowed & (place <= token + (window - shift))
            probs = jnp.where(
                allowed, jnp.exp2(scores[part] * F32(scale * LOG2E) - lse), F32(0.0)
            )
            dscores = (probs * (dprobs[part] - delta)).astype(BF16)
            ds_all[slot, shift : shift + SUB, :] = dscores
            lows.append((probs.astype(BF16), dscores))
        probs_low = jnp.concatenate([x for x, _ in lows], axis=0)
        dscores = jnp.concatenate([x for _, x in lows], axis=0)
        return probs_low, dscores

    def some_blocks(index, nothing):
        blocks = [load(unroll * index + j) for j in range(unroll)]
        stages = [(j, i) for j in range(unroll) for i in range(chunks)]
        ready = front(blocks[0], 0)
        before = jnp.maximum(unroll * index - 1, 0)
        write_query(pl.multiple_of(before * BLOCK, BLOCK), unroll - 1)
        held = None
        for n, (j, i) in enumerate(stages):
            scores, dprobs = ready
            if n + 1 < len(stages):
                jj, ii = stages[n + 1]
                ready = front(blocks[jj], ii)
            if held is not None:
                back(*held)
            if i == 1 and j > 0:
                write_query(blocks[j - 1][0], j - 1)
            held = (blocks[j], i, *middle(blocks[j], j, i, scores, dprobs))
        back(*held)
        return nothing

    lax.fori_loop(0, count // unroll, some_blocks, 0)
    write_query((count - 1) * BLOCK, unroll - 1)

    if closing:
        dk_ref, dv_ref, dk_tail_ref, dv_tail_ref = refs[1:5]
        tail = extent - window
        own = tail - dk_ref.shape[1]
        dk_ref[0] = (dk_all[own:tail] * F32(scale)).astype(BF16)
        dv_ref[0] = dv_all[own:tail].astype(BF16)
        dk_tail_ref[0] = dk_all[tail:] * F32(scale)
        dv_tail_ref[0] = dv_all[tail:]
    else:
        dk_next_ref, dv_next_ref = refs[1:3]
        dk_next_ref[...] = dk_all[extent - window :]
        dv_next_ref[...] = dv_all[extent - window :]
    if opening:
        halo_ref = refs[outputs - 1]
        halo_ref[0, 0] = (dk_all[:window] * F32(scale)).astype(BF16)
        halo_ref[0, 1] = dv_all[:window].astype(BF16)


def head_call(
    head, blocks, me, queries, rims, rim_head, keys, values, lse, start, cotans, before, carry, passing, halos=1
):
    kv_heads, tok_rows, head_dim = keys.shape
    q_heads = queries.shape[0]
    groups = q_heads // kv_heads
    window = rims.shape[2]
    pieces = len(cotans)
    own = tok_rows - window
    first_block, count = blocks
    assert first_block % count == 0
    extent = count * BLOCK + window

    def at_head(*block):
        return pl.BlockSpec(block, lambda i, me: (head, 0, 0))

    def full(*block):
        return pl.BlockSpec(block, lambda i, me: (0,) * len(block))

    q_spec = pl.BlockSpec(
        (groups, count * BLOCK, head_dim), lambda i, me: (head, first_block // count, 0)
    )
    in_specs = [
        q_spec,
        pl.BlockSpec((None, None, window, head_dim), lambda i, me: (0, rim_head, 0, 0)),
        at_head(1, tok_rows, head_dim),
        pl.BlockSpec((None, None, window, head_dim), lambda i, me: (1, rim_head, 0, 0)),
        at_head(1, tok_rows, head_dim),
        full(q_heads, tok_rows),
        full(1, tok_rows),
    ]
    in_specs += [full(*cotans[0].shape)] * pieces
    in_specs += [full(*array.shape) for array in carry]
    in_specs += [pl.BlockSpec(memory_space=pl.ANY)] * (len(before) + len(passing))
    n_in = 1 + 7 + pieces + len(carry)
    unroll = math.gcd(UNROLL, count)
    out_specs = [q_spec]
    out_shape = [jax.ShapeDtypeStruct(queries.shape, BF16)]
    if first_block + count == tok_rows // BLOCK:
        out_specs += [at_head(1, own, head_dim)] * 2 + [at_head(1, window, head_dim)] * 2
        out_shape += [jax.ShapeDtypeStruct(keys.shape, BF16)] * 2
        out_shape += [jax.ShapeDtypeStruct((kv_heads, window, head_dim), F32)] * 2
    else:
        out_specs += [full(window, head_dim)] * 2
        out_shape += [jax.ShapeDtypeStruct((window, head_dim), F32)] * 2
    if first_block == 0:
        at = head if halos > 1 else 0
        out_specs += [pl.BlockSpec((1, 2, window, head_dim), lambda i, me: (at, 0, 0, 0))]
        out_shape += [jax.ShapeDtypeStruct((halos, 2, window, head_dim), BF16)]
    scratch = [
        pltpu.VMEM((extent, head_dim), BF16),
        pltpu.VMEM((extent, head_dim), BF16),
        pltpu.VMEM((head_dim, extent), BF16),
        pltpu.VMEM((groups, tok_rows, head_dim), BF16),
        pltpu.VMEM((tok_rows // BLOCK, 1, groups * BLOCK), F32),
        pltpu.VMEM((unroll, window + BLOCK, groups * BLOCK), BF16),
        pltpu.VMEM((extent, head_dim), F32),
        pltpu.VMEM((extent, head_dim), F32),
    ]
    aliases = {n_in + i: i for i in range(len(before))}
    for i, array in enumerate(passing):
        aliases[n_in + len(before) + i] = len(out_shape)
        out_shape.append(jax.ShapeDtypeStruct(array.shape, array.dtype))
        out_specs.append(pl.BlockSpec(memory_space=pl.ANY))
    pairs = groups * count * BLOCK * (window + BLOCK)
    return pl.pallas_call(
        functools.partial(
            head_kernel, head, blocks, len(carry) // 2, len(before), len(passing)
        ),
        grid_spec=pltpu.PrefetchScalarGridSpec(
            num_scalar_prefetch=1,
            grid=(1,),
            in_specs=in_specs,
            out_specs=out_specs,
            scratch_shapes=scratch,
        ),
        out_shape=out_shape,
        input_output_aliases=aliases,
        compiler_params=pltpu.CompilerParams(vmem_limit_bytes=VMEM_LIMIT),
        cost_estimate=pl.CostEstimate(
            flops=40 * pairs * head_dim, bytes_accessed=8 * tok_rows, transcendentals=0
        ),
        name="head_backward",
    )(me, queries, rims, keys, rims, values, lse, start, *cotans, *carry, *before, *passing)


def join_kernel(joint, dk_tail_ref, dv_tail_ref, *refs):
    backs = refs[:-4]
    dk_ref, dv_ref = refs[-2:]

    def join(back_ref):
        dk_ref[...] = (dk_tail_ref[...] + back_ref[:, 0].astype(F32)).astype(BF16)
        dv_ref[...] = (dv_tail_ref[...] + back_ref[:, 1].astype(F32)).astype(BF16)

    if len(backs) == 1:
        join(backs[0])
    else:
        pl.when(pl.program_id(0) < joint)(lambda: join(backs[0]))
        pl.when(pl.program_id(0) >= joint)(lambda: join(backs[1]))


def join_call(dk_tail, dv_tail, backs, grad_keys, grad_values):
    kv_heads, window, head_dim = dk_tail.shape
    last = grad_keys.shape[1] // window - 1
    joint = backs[0].shape[0]
    tail = pl.BlockSpec((1, window, head_dim), lambda i: (i, 0, 0))
    out = pl.BlockSpec((1, window, head_dim), lambda i: (i, last, 0))
    anywhere = pl.BlockSpec(memory_space=pl.ANY)
    shape = (1, 2, window, head_dim)
    back_specs = [pl.BlockSpec(shape, lambda i: (jnp.minimum(i, joint - 1), 0, 0, 0))]
    back_specs += [pl.BlockSpec(shape, lambda i: (0, 0, 0, 0))] * (len(backs) - 1)
    return pl.pallas_call(
        functools.partial(join_kernel, joint),
        grid=(kv_heads,),
        in_specs=[tail, tail, *back_specs, anywhere, anywhere],
        out_specs=[out, out],
        out_shape=[jax.ShapeDtypeStruct(grad_keys.shape, BF16)] * 2,
        input_output_aliases={2 + len(backs): 0, 3 + len(backs): 1},
        compiler_params=pltpu.CompilerParams(vmem_limit_bytes=VMEM_LIMIT),
        name="join_tails",
    )(dk_tail, dv_tail, *backs, grad_keys, grad_values)


def body(queries, key_states, value_states, attn_output, out_cotangent, logsumexp, doc_start):
    kv_heads, tok_rows, head_dim = key_states.shape
    groups = queries.shape[0] // kv_heads
    pieces = lax.axis_size("head")
    me = lax.axis_index("head").astype(jnp.int32)[None]
    start = doc_start[None, :] - lax.axis_index("ctx") * tok_rows + W
    steps = tok_rows // BLOCK

    def sent(block, distance):
        route = [(i, (i + distance) % pieces) for i in range(pieces)]
        return lax.ppermute(block, "head", route)

    def packed(head, after, *ends):
        return pack_call(
            head, me, out_cotangent, attn_output, kv_heads, groups * head_dim, pieces, after, *ends
        )

    def arrived(parts):
        return [part if k == 0 else sent(part, k) for k, part in enumerate(parts)]

    early = (kv_heads + 1) // 2
    *first, ends = packed(0, out_cotangent, (key_states, value_states), early)
    parts = {0: first}
    cotans = {0: arrived(first)}
    rims = [from_behind(ends, "ctx", 1)]
    after = first[0]
    for head in range(kv_heads - 1, 0, -1):
        parts[head] = packed(head, after)
        after = parts[head][0]
    if kv_heads > 1:
        held = lax.optimization_barrier((*parts[1], *cotans[0][1:]))
        parts[1], cotans[0][1:] = list(held[:pieces]), held[pieces:]
        cotans[1] = arrived(parts[1])
    if kv_heads > early:
        ends = rim_call(key_states, value_states, early, after)
        rims.append(from_behind(ends, "ctx", 1))

    split = 2 * W == tok_rows
    joint = kv_heads - 1 if split else kv_heads
    before = []
    backs = []
    for head in range(kv_heads):
        later = parts[head + 2] if head + 2 < kv_heads else []
        call = functools.partial(
            head_call, head, me=me, queries=queries, rims=rims[head // early], rim_head=head % early,
            keys=key_states, values=value_states, lse=logsumexp, start=start, cotans=cotans[head],
        )
        if head < joint:
            got = call((0, steps), before=before, carry=[], passing=later[1:], halos=joint)
            if later:
                moving = list(got[6:])
                held = lax.optimization_barrier((*[moving[i - 1] for i in (pieces // 2,)], *cotans[head + 1][1:]))
                for i, array in zip((pieces // 2,), held):
                    moving[i - 1] = array
                cotans[head + 1][1:] = held[len((pieces // 2,)) :]
                cotans[head + 2] = arrived([later[0], *moving])
            before = list(got[:6])
            if head == joint - 1:
                backs.append(from_behind(got[5], "ctx", -1))
        else:
            dq, *carry, halo = call((0, steps // 2), before=before[:1], carry=[], passing=[])
            backs.append(from_behind(halo, "ctx", -1))
            before = call((steps // 2, steps // 2), before=[dq, *before[1:5]], carry=carry, passing=[])
    grad_queries, grad_keys, grad_values, *tails = before[:5]
    grad_keys, grad_values = join_call(*tails, backs, grad_keys, grad_values)
    return grad_queries, grad_keys, grad_values


def solution(mesh):
    return jax.shard_map(
        body,
        mesh=mesh,
        in_specs=(
            P("head", "ctx", None),
            P("head", "ctx", None),
            P("head", "ctx", None),
            P(("ctx", "head"), None),
            P(("ctx", "head"), None),
            P("head", "ctx"),
            P("ctx"),
        ),
        out_specs=(P("head", "ctx", None), P("head", "ctx", None), P("head", "ctx", None)),
        check_vma=False,
    )
```

time: 159 us -> 142 us (0.89)
  starting transfers between devices: 49.1 us -> 38.3 us
  waiting for transfers between devices: 6.02 us -> 2.23 us
  local copies, waits for them, and re-layouts: 6.01 us -> 4.29 us
    ppermute x12, starting transfers between devices: 35.6 us -> 26.2 us  [sent(): return lax.ppermute(block, 'head', route)]
    ppermute x5 -> x4, waiting for transfers between devices: 5.98 us -> 0.28 us  [from_behind(): return lax.ppermute(block, axis, route)]
    pallas_call x9 -> x6, Pallas kernels: 24.6 us -> 19.8 us  [the longest x4 12.6 us: pack_call(): pl.pallas_call(functools.partial(pack_kernel, pieces, len(ends)), grid_sp...]
    pallas_call x4 -> x5, Pallas kernels: 70.7 us -> 74.8 us  [head_call(): pl.pallas_call(functools.partial(head_kernel, head, blocks, len(carry) //...]
    ppermute x12, waiting for transfers between devices: 0.03 us -> 1.95 us  [sent(): return lax.ppermute(block, 'head', route)]
    unnamed x40 -> x38, local copies, waits for them, and re-layouts: 6.01 us -> 4.29 us
    ppermute x5 -> x4, starting transfers between devices: 13.5 us -> 12.1 us  [from_behind(): return lax.ppermute(block, axis, route)]
  transfers between devices with their start and end apart: 17 -> 16, of which waited for: 1 -> 2; matrix products, arithmetic and copies ran while one was open for 0% -> 0% of each run, Pallas kernels for 55% -> 61%
where the time goes in v3:
time: 142 us; the launch traced here: 141 us
  Pallas kernels  94.7 us (67%)
  starting transfers between devices  38.3 us (27%)
  local copies, waits for them, and re-layouts  4.29 us (3%)
  waiting for transfers between devices  2.23 us (2%)
    pallas_call x5, Pallas kernels, head_call(): pl.pallas_call(functools.partial(head_kernel, head, blocks, len(carry) //...  74.8 us
    ppermute x12, starting transfers between devices, sent(): return lax.ppermute(block, 'head', route)  26.2 us
    pallas_call x4, Pallas kernels, pack_call(): pl.pallas_call(functools.partial(pack_kernel, pieces, len(ends)), grid_sp...  12.6 us
    ppermute x4, starting transfers between devices, from_behind(): return lax.ppermute(block, axis, route)  12.1 us
    pallas_call x1, Pallas kernels, join_call(): pl.pallas_call(functools.partial(join_kernel, joint), grid=(kv_heads,), i...  4.97 us
    unnamed x38, local copies, waits for them, and re-layouts  4.29 us
  transfers between devices with their start and end apart: 16, of which 2 were waited for; matrix products, arithmetic and copies ran while one was open for 0% of the time, Pallas kernels for 61%

profile of v3, /device:TPU:1, one launch (start us, length us, event | category | flops | bytes accessed | tf_op | source)
XLA Modules:
  0.0 141.0 jit_solution(2650020191804454996)
XLA Ops:
  0.6 3.7 %pack_cotangent.4 = (bf16[528,256]{1,0:T(8,128)(2,1)}, bf16[528,256]{1,0:T(8,128)(2,1)}, bf16[528,256]{1,0:T(8,128)(2,1)}, bf16[528,256]{1,0:T(8,128)(2,1)}, bf16[2,2,1024,128]{3,2,1,0:T(8,128)(2,1)}) custom-call(s32[1]{0:T(128)} %bitcast.me_ref, bf16[512,4096]{1,0:T(8,128)(2,1)} %refs_3_.7, bf16[512,4096]{1,0:T(8,128)(2,1)} %refs_3_.7, ...), custom_call_target="tpu_custom_call" | custom-call | flops 2097152 | bytes 3145728 | tf_op jit(solution)/shard_map/pack_cotangent/pallas_call | solution.py:84
  4.3 4.5 %collective-permute-start.1 = (bf16[2,2,1024,128]{3,2,1,0:T(8,128)(2,1)}, bf16[2,2,1024,128]{3,2,1,0:T(8,128)(2,1)S(1)}, u32[]{:S(2)}, u32[]{:S(2)}) collective-permute-start(bf16[2,2,1024,128]{3,2,1,0:T(8,128)(2,1)} %get-tuple-element.74), channel_id=1, source_target_pairs={{0,4},{4,8},{8,12},{12,16},{16,20},{20,24},{24,28},{1,5},{5,9},{9,... | collective-permute-start | bytes 3145736 | tf_op jit(solution)/shard_map/ppermute | solution.py:27
  8.8 1.3 collective-permute-start.2
  10.2 2.3 %collective-permute-start.3 = (bf16[528,256]{1,0:T(8,128)(2,1)}, bf16[528,256]{1,0:T(8,128)(2,1)S(1)}, u32[]{:S(2)}, u32[]{:S(2)}) collective-permute-start(bf16[528,256]{1,0:T(8,128)(2,1)} %get-tuple-element.79), channel_id=1, source_target_pairs={{0,2},{1,3},{2,0},{3,1},{4,6},{5,7},{6,4},{7,5},{8,10},{9,11},{10,... | collective-permute-start | bytes 811016 | tf_op jit(solution)/shard_map/ppermute | solution.py:406
  13.6 3.0 %pack_cotangent.5 = (bf16[528,256]{1,0:T(8,128)(2,1)}, bf16[528,256]{1,0:T(8,128)(2,1)}, bf16[528,256]{1,0:T(8,128)(2,1)}, bf16[528,256]{1,0:T(8,128)(2,1)}) custom-call(s32[1]{0:T(128)} %bitcast.me_ref, bf16[512,4096]{1,0:T(8,128)(2,1)} %refs_3_.7, bf16[512,4096]{1,0:T(8,128)(2,1)} %refs_3_.7, bf16[512,4096]{1,0:T(8,128)(2,1)} %refs_3_.7, ...), custom_call_target="tpu_custom_call" | custom-call | flops 2097152 | bytes 3145728 | tf_op jit(solution)/shard_map/pack_cotangent/pallas_call | solution.py:84
  16.5 3.0 %pack_cotangent.6 = (bf16[528,256]{1,0:T(8,128)(2,1)}, bf16[528,256]{1,0:T(8,128)(2,1)}, bf16[528,256]{1,0:T(8,128)(2,1)}, bf16[528,256]{1,0:T(8,128)(2,1)}) custom-call(s32[1]{0:T(128)} %bitcast.me_ref, bf16[512,4096]{1,0:T(8,128)(2,1)} %refs_3_.7, bf16[512,4096]{1,0:T(8,128)(2,1)} %refs_3_.7, bf16[512,4096]{1,0:T(8,128)(2,1)} %refs_3_.7, ...), custom_call_target="tpu_custom_call" | custom-call | flops 2097152 | bytes 3145728 | tf_op jit(solution)/shard_map/pack_cotangent/pallas_call | solution.py:84
  19.5 3.0 %pack_cotangent.7 = (bf16[528,256]{1,0:T(8,128)(2,1)}, bf16[528,256]{1,0:T(8,128)(2,1)}, bf16[528,256]{1,0:T(8,128)(2,1)}, bf16[528,256]{1,0:T(8,128)(2,1)}) custom-call(s32[1]{0:T(128)} %bitcast.me_ref, bf16[512,4096]{1,0:T(8,128)(2,1)} %refs_3_.7, bf16[512,4096]{1,0:T(8,128)(2,1)} %refs_3_.7, bf16[512,4096]{1,0:T(8,128)(2,1)} %refs_3_.7, ...), custom_call_target="tpu_custom_call" | custom-call | flops 2097152 | bytes 3145728 | tf_op jit(solution)/shard_map/pack_cotangent/pallas_call | solution.py:84
  22.5 2.2 %rims.1 = bf16[2,2,1024,128]{3,2,1,0:T(8,128)(2,1)} custom-call(bf16[4,2048,128]{2,1,0:T(8,128)(2,1)} %refs_2_.17, bf16[4,2048,128]{2,1,0:T(8,128)(2,1)} %refs_4_.17, bf16[528,256]{1,0:T(8,128)(2,1)} %get-tuple-element.81.after_ref.refs_7_), custom_call_target="tpu_custom_call" | custom-call | tf_op jit(solution)/shard_map/rims/pallas_call | solution.py:110
  24.7 2.7 %collective-permute-start = (bf16[2,2,1024,128]{3,2,1,0:T(8,128)(2,1)}, bf16[2,2,1024,128]{3,2,1,0:T(8,128)(2,1)S(1)}, u32[]{:S(2)}, u32[]{:S(2)}) collective-permute-start(bf16[2,2,1024,128]{3,2,1,0:T(8,128)(2,1)} %rims.1), channel_id=1, source_target_pairs={{0,4},{4,8},{8,12},{12,16},{16,20},{20,24},{24,28},{1,5},{5,9},{9,... | collective-permute-start | bytes 3145736 | tf_op jit(solution)/shard_map/ppermute | solution.py:27
  28.1 1.9 %collective-permute-done.3.refs_9_ = bf16[528,256]{1,0:T(8,128)(2,1)S(1)} collective-permute-done((bf16[528,256]{1,0:T(8,128)(2,1)}, bf16[528,256]{1,0:T(8,128)(2,1)S(1)}, u32[]{:S(2)}, u32[]{:S(2)}) %collective-permute-start.3) | collective-permute-done | bytes 270368 | tf_op jit(solution)/shard_map/ppermute | solution.py:406
  30.0 6.1 %collective-permute-start.5 = (bf16[528,256]{1,0:T(8,128)(2,1)}, bf16[528,256]{1,0:T(8,128)(2,1)S(1)}, u32[]{:S(2)}, u32[]{:S(2)}) collective-permute-start(bf16[528,256]{1,0:T(8,128)(2,1)} %get-tuple-element.89), channel_id=1, source_target_pairs={{0,1},{1,2},{2,3},{3,0},{4,5},{5,6},{6,7},{7,4},{8,9},{9,10},{10,1... | collective-permute-start | bytes 811016 | tf_op jit(solution)/shard_map/ppermute | solution.py:406
  36.1 1.4 collective-permute-start.6
  39.3 17.7 %head_backward.5 = (bf16[8,2048,128]{2,1,0:T(8,128)(2,1)}, bf16[4,2048,128]{2,1,0:T(8,128)(2,1)}, bf16[4,2048,128]{2,1,0:T(8,128)(2,1)}, f32[4,1024,128]{2,1,0:T...) custom-call(s32[1]{0:T(128)} %bitcast.me_ref, ...), custom_call_target="tpu_custom_call", output_to_operand_aliasing={{6}: (12, {}), {7}: (13, {}), {8}: (14, {})} | custom-call | flops 24159191040 | bytes 16384 | tf_op jit(solution)/shard_map/head_backward/pallas_call | solution.py:338
  57.0 4.1 %collective-permute-start.10 = (bf16[528,256]{1,0:T(8,128)(2,1)}, bf16[528,256]{1,0:T(8,128)(2,1)S(1)}, u32[]{:S(2)}, u32[]{:S(2)}) collective-permute-start(bf16[528,256]{1,0:T(8,128)(2,1)} %get-tuple-element.107), channel_id=1, source_target_pairs={{0,2},{1,3},{2,0},{3,1},{4,6},{5,7},{6,4},{7,5},{8,10},{9,11},{10,... | collective-permute-start | bytes 811016 | tf_op jit(solution)/shard_map/ppermute | solution.py:406
  61.0 3.1 %collective-permute-start.11 = (bf16[528,256]{1,0:T(8,128)(2,1)}, bf16[528,256]{1,0:T(8,128)(2,1)S(1)}, u32[]{:S(2)}, u32[]{:S(2)}) collective-permute-start(bf16[528,256]{1,0:T(8,128)(2,1)} %get-tuple-element.108), channel_id=1, source_target_pairs={{0,3},{1,0},{2,1},{3,2},{4,7},{5,4},{6,5},{7,6},{8,11},{9,8},{10,9... | collective-permute-start | bytes 811016 | tf_op jit(solution)/shard_map/ppermute | solution.py:406
  64.2 17.7 %head_backward.6 = (bf16[8,2048,128]{2,1,0:T(8,128)(2,1)}, bf16[4,2048,128]{2,1,0:T(8,128)(2,1)}, bf16[4,2048,128]{2,1,0:T(8,128)(2,1)}, f32[4,1024,128]{2,1,0:T...) custom-call(s32[1]{0:T(128)} %bitcast.me_ref, ...), custom_call_target="tpu_custom_call", output_to_operand_aliasing={{0}: (12, {}), {1}: (13, {}), {2}: (14, {}), {3}: (15, {}),... | custom-call | flops 24159191040 | bytes 16384 | tf_op jit(solution)/shard_map/head_backward/pallas_call | solution.py:338
  81.9 3.2 %collective-permute-start.13 = (bf16[528,256]{1,0:T(8,128)(2,1)}, bf16[528,256]{1,0:T(8,128)(2,1)S(1)}, u32[]{:S(2)}, u32[]{:S(2)}) collective-permute-start(bf16[528,256]{1,0:T(8,128)(2,1)} %get-tuple-element.110), channel_id=1, source_target_pairs={{0,3},{1,0},{2,1},{3,2},{4,7},{5,4},{6,5},{7,6},{8,11},{9,8},{10,9... | collective-permute-start | bytes 811016 | tf_op jit(solution)/shard_map/ppermute | solution.py:406
  85.2 2.8 %collective-permute-start.12 = (bf16[528,256]{1,0:T(8,128)(2,1)}, bf16[528,256]{1,0:T(8,128)(2,1)S(1)}, u32[]{:S(2)}, u32[]{:S(2)}) collective-permute-start(bf16[528,256]{1,0:T(8,128)(2,1)} %get-tuple-element.109), channel_id=1, source_target_pairs={{0,2},{1,3},{2,0},{3,1},{4,6},{5,7},{6,4},{7,5},{8,10},{9,11},{10,... | collective-permute-start | bytes 811016 | tf_op jit(solution)/shard_map/ppermute | solution.py:406
  89.1 17.7 %head_backward.7 = (bf16[8,2048,128]{2,1,0:T(8,128)(2,1)}, bf16[4,2048,128]{2,1,0:T(8,128)(2,1)}, bf16[4,2048,128]{2,1,0:T(8,128)(2,1)}, f32[4,1024,128]{2,1,0:T...) custom-call(s32[1]{0:T(128)} %bitcast.me_ref, ...), custom_call_target="tpu_custom_call", output_to_operand_aliasing={{0}: (12, {}), {1}: (13, {}), {2}: (14, {}), {3}: (15, {}),... | custom-call | flops 24159191040 | bytes 16384 | tf_op jit(solution)/shard_map/head_backward/pallas_call | solution.py:338
  106.7 3.0 %collective-permute-start.14 = (bf16[3,2,1024,128]{3,2,1,0:T(8,128)(2,1)}, bf16[3,2,1024,128]{3,2,1,0:T(8,128)(2,1)S(1)}, u32[]{:S(2)}, u32[]{:S(2)}) collective-permute-start(bf16[3,2,1024,128]{3,2,1,0:T(8,128)(2,1)} %get-tuple-element.131), channel_id=1, source_target_pairs={{4,0},{8,4},{12,8},{16,12},{20,16},{24,20},{28,24},{5,1},{9,5},{13... | collective-permute-start | bytes 4718600 | tf_op jit(solution)/shard_map/ppermute | solution.py:27
  110.6 10.7 %head_backward.8 = (bf16[8,2048,128]{2,1,0:T(8,128)(2,1)}, f32[1024,128]{1,0:T(8,128)}, f32[1024,128]{1,0:T(8,128)}, bf16[1,2,1024,128]{3,2,1,0:T(8,128)(2,1)}) custom-call(s32[1]{0:T(128)} %bitcast.me_ref, bf16[8,2048,128]{2,1,0:T(8,128)(2,1)} %refs_0_.17, bf16[2,2,1024,128]{3,2,1,0:T(8,128)(2,1)} %copy-done.3, ...), custom_call_target="tpu_custom_call", output_to_operand_aliasing={{0}: (12, {})} | custom-call | flops 12079595520 | bytes 16384 | tf_op jit(solution)/shard_map/head_backward/pallas_call | solution.py:338
  121.3 1.9 %collective-permute-start.15 = (bf16[1,2,1024,128]{3,2,1,0:T(8,128)(2,1)}, bf16[1,2,1024,128]{3,2,1,0:T(8,128)(2,1)S(1)}, u32[]{:S(2)}, u32[]{:S(2)}) collective-permute-start(bf16[1,2,1024,128]{3,2,1,0:T(8,128)(2,1)} %get-tuple-element.132), channel_id=1, source_target_pairs={{4,0},{8,4},{12,8},{16,12},{20,16},{24,20},{28,24},{5,1},{9,5},{13... | collective-permute-start | bytes 1572872 | tf_op jit(solution)/shard_map/ppermute | solution.py:27
  123.2 11.1 %head_backward.9 = (bf16[8,2048,128]{2,1,0:T(8,128)(2,1)}, bf16[4,2048,128]{2,1,0:T(8,128)(2,1)}, bf16[4,2048,128]{2,1,0:T(8,128)(2,1)}, f32[4,1024,128]{2,1,0:T(8,128)}, f32[4,1024,128]{2,1,0:T(8,128)}) custom-call(s32[1]{0:T(128)} %bitcast.me_ref, ...), custom_call_target="tpu_custom_call", output_to_operand_aliasing={{0}: (14, {}), {1}: (15, {}), {2}: (16, {}), {3}: (17, {}),... | custom-call | flops 12079595520 | bytes 16384 | tf_op jit(solution)/shard_map/head_backward/pallas_call | solution.py:338
  136.0 5.0 %join_tails.1 = (bf16[4,2048,128]{2,1,0:T(8,128)(2,1)}, bf16[4,2048,128]{2,1,0:T(8,128)(2,1)}) custom-call(f32[4,1024,128]{2,1,0:T(8,128)} %get-tuple-element.129.dk_tail_ref, f32[4,1024,128]{2,1,0:T(8,128)} %get-tuple-element.130.dv_tail_ref, bf16[3,2,1024,128]{3,2,1,0:T(8,128)(2,1)} %copy-done, ...), custom_call_target="tpu_custom_call", output_to_operand_aliasing={{0}: (4, {}), {1}: (5, {})} | custom-call | tf_op jit(solution)/shard_map/join_tails/pallas_call | solution.py:384
  (58 shorter events, 7.0 us)
Async XLA Ops:
  4.3 33.9 %collective-permute-start.1 = (bf16[2,2,1024,128]{3,2,1,0:T(8,128)(2,1)}, bf16[2,2,1024,128]{3,2,1,0:T(8,128)(2,1)S(1)}, u32[]{:S(2)}, u32[]{:S(2)}) collective-permute-start(bf16[2,2,1024,128]{3,2,1,0:T(8,128)(2,1)} %get-tuple-element.74), channel_id=1, source_target_pairs={{0,4},{4,8},{8,12},{12,16},{16,20},{20,24},{24,28},{1,5},{5,9},{9,... | collective-permute-start | bytes 3145736 | tf_op jit(solution)/shard_map/ppermute | solution.py:27
  8.8 19.3 %collective-permute-start.2 = (bf16[528,256]{1,0:T(8,128)(2,1)}, bf16[528,256]{1,0:T(8,128)(2,1)S(1)}, u32[]{:S(2)}, u32[]{:S(2)}) collective-permute-start(bf16[528,256]{1,0:T(8,128)(2,1)} %get-tuple-element.78), channel_id=1, source_target_pairs={{0,1},{1,2},{2,3},{3,0},{4,5},{5,6},{6,7},{7,4},{8,9},{9,10},{10,1... | collective-permute-start | bytes 811016 | tf_op jit(solution)/shard_map/ppermute | solution.py:406
  10.2 19.8 %collective-permute-start.3 = (bf16[528,256]{1,0:T(8,128)(2,1)}, bf16[528,256]{1,0:T(8,128)(2,1)S(1)}, u32[]{:S(2)}, u32[]{:S(2)}) collective-permute-start(bf16[528,256]{1,0:T(8,128)(2,1)} %get-tuple-element.79), channel_id=1, source_target_pairs={{0,2},{1,3},{2,0},{3,1},{4,6},{5,7},{6,4},{7,5},{8,10},{9,11},{10,... | collective-permute-start | bytes 811016 | tf_op jit(solution)/shard_map/ppermute | solution.py:406
  12.5 17.5 %collective-permute-start.4 = (bf16[528,256]{1,0:T(8,128)(2,1)}, bf16[528,256]{1,0:T(8,128)(2,1)S(1)}, u32[]{:S(2)}, u32[]{:S(2)}) collective-permute-start(bf16[528,256]{1,0:T(8,128)(2,1)} %get-tuple-element.80), channel_id=1, source_target_pairs={{0,3},{1,0},{2,1},{3,2},{4,7},{5,4},{6,5},{7,6},{8,11},{9,8},{10,9... | collective-permute-start | bytes 811016 | tf_op jit(solution)/shard_map/ppermute | solution.py:406
  22.5 13.6 %copy-start.11 = (bf16[528,256]{1,0:T(8,128)(2,1)S(1)}, bf16[528,256]{1,0:T(8,128)(2,1)}, u32[]{:S(2)}) copy-start(bf16[528,256]{1,0:T(8,128)(2,1)} %get-tuple-element.90) | copy-start | bytes 811012
  22.5 15.0 %copy-start.9 = (bf16[528,256]{1,0:T(8,128)(2,1)S(1)}, bf16[528,256]{1,0:T(8,128)(2,1)}, u32[]{:S(2)}) copy-start(bf16[528,256]{1,0:T(8,128)(2,1)} %get-tuple-element.91) | copy-start | bytes 811012
  24.7 63.3 %collective-permute-start = (bf16[2,2,1024,128]{3,2,1,0:T(8,128)(2,1)}, bf16[2,2,1024,128]{3,2,1,0:T(8,128)(2,1)S(1)}, u32[]{:S(2)}, u32[]{:S(2)}) collective-permute-start(bf16[2,2,1024,128]{3,2,1,0:T(8,128)(2,1)} %rims.1), channel_id=1, source_target_pairs={{0,4},{4,8},{8,12},{12,16},{16,20},{20,24},{24,28},{1,5},{5,9},{9,... | collective-permute-start | bytes 3145736 | tf_op jit(solution)/shard_map/ppermute | solution.py:27
  28.1 10.2 %copy-start.5 = (bf16[528,256]{1,0:T(8,128)(2,1)}, bf16[528,256]{1,0:T(8,128)(2,1)S(1)}, u32[]{:S(2)}) copy-start(bf16[528,256]{1,0:T(8,128)(2,1)S(1)} %collective-permute-done.2.refs_8_) | copy-start | bytes 811012
  30.0 8.2 %copy-start.6 = (bf16[528,256]{1,0:T(8,128)(2,1)}, bf16[528,256]{1,0:T(8,128)(2,1)S(1)}, u32[]{:S(2)}) copy-start(bf16[528,256]{1,0:T(8,128)(2,1)S(1)} %collective-permute-done.3.refs_9_) | copy-start | bytes 811012
  30.0 8.2 %copy-start.8 = (bf16[528,256]{1,0:T(8,128)(2,1)}, bf16[528,256]{1,0:T(8,128)(2,1)S(1)}, u32[]{:S(2)}) copy-start(bf16[528,256]{1,0:T(8,128)(2,1)S(1)} %collective-permute-done.4.refs_10_) | copy-start | bytes 811012
  30.0 26.9 %collective-permute-start.5 = (bf16[528,256]{1,0:T(8,128)(2,1)}, bf16[528,256]{1,0:T(8,128)(2,1)S(1)}, u32[]{:S(2)}, u32[]{:S(2)}) collective-permute-start(bf16[528,256]{1,0:T(8,128)(2,1)} %get-tuple-element.89), channel_id=1, source_target_pairs={{0,1},{1,2},{2,3},{3,0},{4,5},{5,6},{6,7},{7,4},{8,9},{9,10},{10,1... | collective-permute-start | bytes 811016 | tf_op jit(solution)/shard_map/ppermute | solution.py:406
  36.1 20.8 %collective-permute-start.6 = (bf16[528,256]{1,0:T(8,128)(2,1)S(1)}, bf16[528,256]{1,0:T(8,128)(2,1)S(1)}, u32[]{:S(2)}, u32[]{:S(2)}) collective-permute-start(bf16[528,256]{1,0:T(8,128)(2,1)S(1)} %copy-done.11), channel_id=1, source_target_pairs={{0,2},{1,3},{2,0},{3,1},{4,6},{5,7},{6,4},{7,5},{8,10},{9,11},{10,... | collective-permute-start | bytes 811016 | tf_op jit(solution)/shard_map/ppermute | solution.py:406
  37.5 19.5 %collective-permute-start.7 = (bf16[528,256]{1,0:T(8,128)(2,1)S(1)}, bf16[528,256]{1,0:T(8,128)(2,1)S(1)}, u32[]{:S(2)}, u32[]{:S(2)}) collective-permute-start(bf16[528,256]{1,0:T(8,128)(2,1)S(1)} %copy-done.9), channel_id=1, source_target_pairs={{0,3},{1,0},{2,1},{3,2},{4,7},{5,4},{6,5},{7,6},{8,11},{9,8},{10,9... | collective-permute-start | bytes 811016 | tf_op jit(solution)/shard_map/ppermute | solution.py:406
  56.9 7.2 %copy-start.12 = (bf16[528,256]{1,0:T(8,128)(2,1)}, bf16[528,256]{1,0:T(8,128)(2,1)S(1)}, u32[]{:S(2)}) copy-start(bf16[528,256]{1,0:T(8,128)(2,1)S(1)} %collective-permute-done.5.refs_8_) | copy-start | bytes 811012
  56.9 7.2 %copy-start.14 = (bf16[528,256]{1,0:T(8,128)(2,1)}, bf16[528,256]{1,0:T(8,128)(2,1)S(1)}, u32[]{:S(2)}) copy-start(bf16[528,256]{1,0:T(8,128)(2,1)S(1)} %collective-permute-done.6.refs_9_) | copy-start | bytes 811012
  57.0 7.2 %copy-start.16 = (bf16[528,256]{1,0:T(8,128)(2,1)}, bf16[528,256]{1,0:T(8,128)(2,1)S(1)}, u32[]{:S(2)}) copy-start(bf16[528,256]{1,0:T(8,128)(2,1)S(1)} %collective-permute-done.7.refs_10_) | copy-start | bytes 811012
  57.0 28.1 %collective-permute-start.10 = (bf16[528,256]{1,0:T(8,128)(2,1)}, bf16[528,256]{1,0:T(8,128)(2,1)S(1)}, u32[]{:S(2)}, u32[]{:S(2)}) collective-permute-start(bf16[528,256]{1,0:T(8,128)(2,1)} %get-tuple-element.107), channel_id=1, source_target_pairs={{0,2},{1,3},{2,0},{3,1},{4,6},{5,7},{6,4},{7,5},{8,10},{9,11},{10,... | collective-permute-start | bytes 811016 | tf_op jit(solution)/shard_map/ppermute | solution.py:406
  61.0 24.1 %collective-permute-start.11 = (bf16[528,256]{1,0:T(8,128)(2,1)}, bf16[528,256]{1,0:T(8,128)(2,1)S(1)}, u32[]{:S(2)}, u32[]{:S(2)}) collective-permute-start(bf16[528,256]{1,0:T(8,128)(2,1)} %get-tuple-element.108), channel_id=1, source_target_pairs={{0,3},{1,0},{2,1},{3,2},{4,7},{5,4},{6,5},{7,6},{8,11},{9,8},{10,9... | collective-permute-start | bytes 811016 | tf_op jit(solution)/shard_map/ppermute | solution.py:406
  64.1 21.0 %collective-permute-start.9 = (bf16[528,256]{1,0:T(8,128)(2,1)}, bf16[528,256]{1,0:T(8,128)(2,1)S(1)}, u32[]{:S(2)}, u32[]{:S(2)}) collective-permute-start(bf16[528,256]{1,0:T(8,128)(2,1)} %get-tuple-element.106), channel_id=1, source_target_pairs={{0,1},{1,2},{2,3},{3,0},{4,5},{5,6},{6,7},{7,4},{8,9},{9,10},{10,1... | collective-permute-start | bytes 811016 | tf_op jit(solution)/shard_map/ppermute | solution.py:406
  81.9 27.9 %collective-permute-start.13 = (bf16[528,256]{1,0:T(8,128)(2,1)}, bf16[528,256]{1,0:T(8,128)(2,1)S(1)}, u32[]{:S(2)}, u32[]{:S(2)}) collective-permute-start(bf16[528,256]{1,0:T(8,128)(2,1)} %get-tuple-element.110), channel_id=1, source_target_pairs={{0,3},{1,0},{2,1},{3,2},{4,7},{5,4},{6,5},{7,6},{8,11},{9,8},{10,9... | collective-permute-start | bytes 811016 | tf_op jit(solution)/shard_map/ppermute | solution.py:406
  85.1 24.6 %collective-permute-start.8 = (bf16[528,256]{1,0:T(8,128)(2,1)}, bf16[528,256]{1,0:T(8,128)(2,1)S(1)}, u32[]{:S(2)}, u32[]{:S(2)}) collective-permute-start(bf16[528,256]{1,0:T(8,128)(2,1)} %get-tuple-element.104), channel_id=1, source_target_pairs={{0,1},{1,2},{2,3},{3,0},{4,5},{5,6},{6,7},{7,4},{8,9},{9,10},{10,1... | collective-permute-start | bytes 811016 | tf_op jit(solution)/shard_map/ppermute | solution.py:406
  85.2 24.6 %collective-permute-start.12 = (bf16[528,256]{1,0:T(8,128)(2,1)}, bf16[528,256]{1,0:T(8,128)(2,1)S(1)}, u32[]{:S(2)}, u32[]{:S(2)}) collective-permute-start(bf16[528,256]{1,0:T(8,128)(2,1)} %get-tuple-element.109), channel_id=1, source_target_pairs={{0,2},{1,3},{2,0},{3,1},{4,6},{5,7},{6,4},{7,5},{8,10},{9,11},{10,... | collective-permute-start | bytes 811016 | tf_op jit(solution)/shard_map/ppermute | solution.py:406
  106.7 27.9 %collective-permute-start.14 = (bf16[3,2,1024,128]{3,2,1,0:T(8,128)(2,1)}, bf16[3,2,1024,128]{3,2,1,0:T(8,128)(2,1)S(1)}, u32[]{:S(2)}, u32[]{:S(2)}) collective-permute-start(bf16[3,2,1024,128]{3,2,1,0:T(8,128)(2,1)} %get-tuple-element.131), channel_id=1, source_target_pairs={{4,0},{8,4},{12,8},{16,12},{20,16},{24,20},{28,24},{5,1},{9,5},{13... | collective-permute-start | bytes 4718600 | tf_op jit(solution)/shard_map/ppermute | solution.py:27
  121.3 13.3 %collective-permute-start.15 = (bf16[1,2,1024,128]{3,2,1,0:T(8,128)(2,1)}, bf16[1,2,1024,128]{3,2,1,0:T(8,128)(2,1)S(1)}, u32[]{:S(2)}, u32[]{:S(2)}) collective-permute-start(bf16[1,2,1024,128]{3,2,1,0:T(8,128)(2,1)} %get-tuple-element.132), channel_id=1, source_target_pairs={{4,0},{8,4},{12,8},{16,12},{20,16},{24,20},{28,24},{5,1},{9,5},{13... | collective-permute-start | bytes 1572872 | tf_op jit(solution)/shard_map/ppermute | solution.py:27
  (11 other events, 20.2 us)
